TPU v7x, 32 devices: a whole 2x2x4 slice. The times are simulated.
32 devices in a mesh: tok: 4 (over y, core), head: 8 (over z, x).
Axes of the slice: x: 2, y: 2, z: 4, core: 2. Of those that a mesh axis runs over, the one named last changes fastest.
Arguments:
- hidden_states: bfloat16 [2560, 6144], P('tok', 'head'), may hold values from -6 to 6
- norm_gain: float32 [6144], replicated, may hold values from 0.5 to 1.5
- norm_bias: float32 [6144], replicated, may hold values from -2 to 2
- qkv_weight: bfloat16 [6144, 18432], P('tok', 'head'), may hold values from -0.125 to 0.125
- qkv_bias: bfloat16 [18432], P('head'), may hold values from -2 to 2
- dense_weight: bfloat16 [6144, 6144], P('head'), may hold values from -0.21875 to 0.21875
- dense_bias: bfloat16 [6144], P('head'), may hold values from -2 to 2
- prefix_keys: bfloat16 [8, 2048, 6144], P('tok', None, 'head'), may hold values from -70 to 70
- prefix_values: bfloat16 [8, 2048, 6144], P('tok', None, 'head'), may hold values from -10 to 10
- suffix_len: int32 [4, 8], P('tok'), may hold values from 1 to 240, as said below
- request_order: int32 [4, 8], P('tok'), may hold values from 0 to 7, each once within a row
- group_slot: int32 [8], replicated, may hold values from 0 to 7, each once
Outputs:
- layer_out: bfloat16 [2560, 6144], P('tok', 'head')
Inputs may be any that keep to these rules, and one draw needn't show every extreme that they name: `suffix_len`: each row sums to 640; one group, the same in every row, has exactly 240 in every row. `request_order`: each row names every group once. `group_slot`: each slot holds one group.
All inputs are finite; a program needn't handle non-finite values.
Results may differ from a plain program's by a relative error of at most 0.007.
The roundings to bfloat16 on the way count: a program that leaves them out, or rounds other values in their place, can miss the bound.
Values may be sent and summed in bfloat16 or wider, within the bound.
No kernel may reach another device: no remote copies, remote signals or barrier semaphores. Data moves between devices by JAX's collectives and lax.ppermute only.
A program may use at most 192 MiB of HBM per device.

v0:
```python
import jax
import jax.numpy as jnp
from jax import lax
from jax.sharding import PartitionSpec as P

HS = 96


def layer_norm(values_in, gain, shift):
    widened = values_in.astype(jnp.float32)
    center = jnp.mean(widened, axis=-1, keepdims=True)
    spread = jnp.mean(jnp.square(widened - center), axis=-1, keepdims=True)
    return ((widened - center) * lax.rsqrt(spread + 1e-05) * gain + shift).astype(jnp.bfloat16)


def shard_layout(lengths, ordering, row_count):
    group_count = lengths.shape[0]
    labels = jnp.arange(group_count, dtype=jnp.int32)
    chosen = (ordering[:, None] == labels[None, :]).astype(jnp.int32)
    ranking = jnp.sum(labels[:, None] * chosen, axis=0)
    earlier = (ranking[None, :] < ranking[:, None]).astype(jnp.int32)
    starts = jnp.sum(earlier * lengths[None, :], axis=1)
    places = jnp.arange(row_count, dtype=jnp.int32)
    member = (
        (places[:, None] >= starts[None, :]) & (places[:, None] < (starts + lengths)[None, :])
    ).astype(jnp.int32)
    group_of = jnp.sum(member * labels[None, :], axis=1)
    within = places - jnp.sum(member * starts[None, :], axis=1)
    return (starts, member, group_of, within)


def rotary(tensor, positions, rot_dims):
    half_dims = rot_dims // 2
    inverse = 10000.0 ** (-(jnp.arange(half_dims, dtype=jnp.float32) * 2.0) / rot_dims)
    angles = positions.astype(jnp.float32)[:, None] * inverse[None, :]
    cosine = jnp.cos(angles)[:, None, :]
    sine_part = jnp.sin(angles)[:, None, :]
    lower_half = tensor[..., :half_dims]
    upper_half = tensor[..., half_dims:rot_dims]
    return jnp.concatenate(
        [
            lower_half * cosine - upper_half * sine_part,
            upper_half * cosine + lower_half * sine_part,
            tensor[..., rot_dims:],
        ],
        axis=-1,
    )


def local_suffix(queries, keys_new, values_new, group_of):
    scaling = HS ** (-0.5)
    scores = (
        jnp.einsum("ihd,jhd->hij", queries, keys_new, preferred_element_type=jnp.float32) * scaling
    )
    places = jnp.arange(queries.shape[0], dtype=jnp.int32)
    allowed = (group_of[:, None] == group_of[None, :]) & (places[None, :] <= places[:, None])
    masked = jnp.where(allowed[None], scores, -jnp.inf)
    row_peak = jnp.max(masked, axis=-1)
    weights = jnp.exp(masked - row_peak[..., None])
    row_mass = jnp.sum(weights, axis=-1)
    blended = (
        jnp.einsum(
            "hij,jhd->ihd",
            weights.astype(jnp.bfloat16),
            values_new,
            preferred_element_type=jnp.float32,
        )
        / jnp.transpose(row_mass)[..., None]
    )
    return (jnp.transpose(row_peak), jnp.transpose(row_mass), blended)


def prefix_slot(operands):
    queries_in, keys_in, values_in = operands
    row_total = queries_in.shape[0]
    local_width = queries_in.shape[1]
    local_heads = local_width // HS
    prefix_length = keys_in.shape[0]
    query_heads = queries_in.reshape(row_total, local_heads, HS)
    key_heads = keys_in.reshape(prefix_length, local_heads, HS)
    value_heads = values_in.reshape(prefix_length, local_heads, HS)
    scores = jnp.einsum(
        "rhd,phd->hrp", query_heads, key_heads, preferred_element_type=jnp.float32
    ) * HS ** (-0.5)
    row_peak = jnp.max(scores, axis=-1)
    weights = jnp.exp(scores - row_peak[..., None])
    row_mass = jnp.sum(weights, axis=-1)
    blended = (
        jnp.einsum(
            "hrp,phd->rhd",
            weights.astype(jnp.bfloat16),
            value_heads,
            preferred_element_type=jnp.float32,
        )
        / jnp.transpose(row_mass)[..., None]
    )
    return (
        blended.reshape(row_total, local_width),
        jnp.transpose(row_peak),
        jnp.transpose(row_mass),
    )


def on_device(
    hidden_states,
    norm_gain,
    norm_bias,
    qkv_weight,
    qkv_bias,
    dense_weight,
    dense_bias,
    prefix_keys,
    prefix_values,
    suffix_len,
    request_order,
    group_slot,
):
    tok_rows = hidden_states.shape[0]
    slot_local = prefix_keys.shape[0]
    prefix_length = prefix_keys.shape[1]
    local_width = prefix_keys.shape[2]
    local_heads = local_width // HS
    group_count = slot_local * lax.axis_size("tok")
    capacity = 3 * tok_rows // group_count
    full_rows = lax.all_gather(hidden_states, "head", axis=1, tiled=True)
    normed = layer_norm(full_rows, norm_gain, norm_bias)
    projected = jnp.dot(
        normed,
        lax.all_gather(qkv_weight, "tok", axis=0, tiled=True),
        preferred_element_type=jnp.float32,
    )
    projected = (projected + qkv_bias.astype(jnp.float32)).reshape(tok_rows, local_heads, 3, HS)
    lengths = suffix_len[0]
    starts, member, group_of, within = shard_layout(lengths, request_order[0], tok_rows)
    positions = prefix_length + within
    queries = rotary(projected[:, :, 0], positions, HS // 4).astype(jnp.bfloat16)
    keys_new = rotary(projected[:, :, 1], positions, HS // 4).astype(jnp.bfloat16)
    values_new = projected[:, :, 2].astype(jnp.bfloat16)
    suf_peak, suf_mass, suf_out = local_suffix(queries, keys_new, values_new, group_of)
    labels = jnp.arange(group_count, dtype=jnp.int32)
    slot_match = (group_slot[:, None] == labels[None, :]).astype(jnp.int32)
    slot_starts = jnp.sum(starts[:, None] * slot_match, axis=0)
    slot_lengths = jnp.sum(lengths[:, None] * slot_match, axis=0)
    cap_index = jnp.arange(capacity, dtype=jnp.int32)
    live_slot = cap_index[None, :] < slot_lengths[:, None]
    source_rows = jnp.where(live_slot, slot_starts[:, None] + cap_index[None, :], 0)
    flat_query = queries.reshape(tok_rows, local_width)
    outgoing = jnp.where(live_slot[..., None], flat_query[source_rows], jnp.zeros((), jnp.bfloat16))
    incoming = lax.all_to_all(outgoing, "tok", split_axis=0, concat_axis=1, tiled=True)
    pre_all, peak_all, mass_all = lax.map(prefix_slot, (incoming, prefix_keys, prefix_values))
    returned = (
        lax.all_to_all(pre_all, "tok", split_axis=1, concat_axis=0, tiled=True),
        lax.all_to_all(peak_all, "tok", split_axis=1, concat_axis=0, tiled=True),
        lax.all_to_all(mass_all, "tok", split_axis=1, concat_axis=0, tiled=True),
    )
    token_slot = jnp.sum(member * group_slot[None, :], axis=1)
    flat_index = token_slot * capacity + within
    pre_out = returned[0].reshape(group_count * capacity, local_heads, HS)[flat_index]
    pre_peak = returned[1].reshape(group_count * capacity, local_heads)[flat_index]
    pre_mass = returned[2].reshape(group_count * capacity, local_heads)[flat_index]
    joint_peak = jnp.maximum(pre_peak, suf_peak)
    pre_share = pre_mass * jnp.exp(pre_peak - joint_peak)
    suf_share = suf_mass * jnp.exp(suf_peak - joint_peak)
    combined = (pre_share[..., None] * pre_out + suf_share[..., None] * suf_out) / (
        pre_share + suf_share
    )[..., None]
    attention = combined.reshape(tok_rows, local_width).astype(jnp.bfloat16)
    partial_out = jnp.dot(attention, dense_weight, preferred_element_type=jnp.float32)
    summed = lax.psum_scatter(partial_out, "head", scatter_dimension=1, tiled=True)
    return (hidden_states.astype(jnp.float32) + dense_bias.astype(jnp.float32) + summed).astype(
        jnp.bfloat16
    )


def solution(mesh):
    placed = (
        P("tok", "head"),
        P(),
        P(),
        P("tok", "head"),
        P("head"),
        P("head", None),
        P("head"),
        P("tok", None, "head"),
        P("tok", None, "head"),
        P("tok", None),
        P("tok", None),
        P(),
    )
    return jax.shard_map(
        on_device, mesh=mesh, in_specs=placed, out_specs=P("tok", "head"), check_vma=False
    )
```

profile of v0, /device:TPU:14, one launch (start us, length us, event | category | flops | bytes accessed | tf_op | source)
XLA Modules:
  0.0 1065.5 jit_solution(13411627849760154682)
XLA Ops:
  7.3 0.7 all-gather.5.cloned.1.call-update
  10.2 116.9 %all-gather.3.cloned.1.call-done = bf16[640,6144]{1,0:T(8,128)(2,1)} async-done(((bf16[640,768]{1,0:T(8,128)(2,1)}), bf16[640,6144]{1,0:T(8,128)(2,1)}) %all-gather.3.cloned.1.call-update) | async-done | bytes 7864336 | tf_op jit(solution)/shard_map/all_gather | solution.py:125
  127.1 4.5 convert_reduce_fusion
  131.7 0.9 copy-done.1
  132.6 2.2 fusion.9
  134.8 165.5 %all-gather.5.cloned.1.call-done = bf16[6144,2304]{1,0:T(8,128)(2,1)} async-done(((bf16[1536,2304]{1,0:T(8,128)(2,1)}), bf16[6144,2304]{1,0:T(8,128)(2,1)}) %all-gather.5.cloned.1.call-update) | async-done | bytes 28311568 | tf_op jit(solution)/shard_map/all_gather | solution.py:129
  300.3 28.7 %fusion.25 = f32[640,2304]{1,0:T(8,128)} fusion(bf16[6144,2304]{1,0:T(8,128)(2,1)} %all-gather.5.cloned.1.call-done, bf16[640,6144]{1,0:T(8,128)(2,1)} %all-gather.3.cloned.1.call-done, f32[6144]{0:T(1024)S(1)} %copy-done.22, f32[6144]{0:T(1024)S(1)} %copy-done.23, f32[640]{0:T(1024)S(1)} %add_rsqrt_fusion, f32[640]{0:T(1024)S(1)} %broadcast_multiply_fusion.1, ...), kind=kOutput, calls=%fused_computation.36 | convolution fusion | flops 18144460800 | bytes 42137600 | tf_op jit(solution)/shard_map/dot_general | solution.py:127
  329.0 7.7 copy.119
  336.7 2.4 fusion.56
  339.2 1.5 copy_bitcast_fusion
  341.7 7.0 gather_fusion
  348.8 3.2 broadcast_select_fusion
  351.9 5.3 all-to-all-start
  357.2 33.1 %all-to-all-done = bf16[8,240,768]{2,1,0:T(8,128)(2,1)S(1)} async-done(((bf16[8,240,768]{2,1,0:T(8,128)(2,1)}), bf16[8,240,768]{2,1,0:T(8,128)(2,1)S(1)}, u32[]{:S(2)}, u32[]{:S(2)}) %all-to-all-start) | async-done | bytes 2949152 | tf_op jit(solution)/shard_map/all_to_all | solution.py:149
  390.4 1.8 copy.122
  392.1 281.3 %while.14 = (s32[]{:T(128)}, f32[2,960,768]{2,0,1:T(2,128)}, f32[2,960,8]{1,2,0:T(8,128)S(1)}, f32[2,960,8]{1,2,0:T(8,128)S(1)}, bf16[2,2048,768]{2,1,0:T(8,128)...) while((s32[]{:T(128)}, f32[2,960,768]{2,0,1:T(2,128)}, ...), condition=%wide.region_10.11_spmd, body=%wide.region_7.10_spmd.sunk | while | flops 6166348800 | bytes 255187088 | solution.py:150
  392.1 1.5 constant_dynamic-slice_fusion.7
  393.6 1.6 copy.166
  395.2 2.1 constant_dynamic-slice_fusion.8
  397.3 3.0 copy.167
  400.3 2.1 constant_dynamic-slice_fusion.6
  402.4 3.0 copy.165
  405.4 24.0 %multiply_reduce_fusion.2 = (f32[8,960]{1,0:T(8,128)S(1)}, f32[8,960,2048]{2,1,0:T(8,128)}) fusion(bf16[960,8,96]{0,2,1:T(8,128)(2,1)} %bitcast.102, bf16[2048,8,96]{0,2,1:T(8,128)(2,1)} %bitcast.101), kind=kOutput, calls=%fused_computation.5.clone.1 | convolution fusion | flops 3051348480 | bytes 67565568 | tf_op jit(solution)/shard_map/while/body/eval_jaxpr/rhd,phd->hrp/dot_general | solution.py:82
  429.4 20.2 %fusion.75 = f32[8,960]{1,0:T(8,128)S(1)} fusion(f32[8,960,2048]{2,1,0:T(8,128)} %get-tuple-element.176, f32[8,960]{1,0:T(8,128)S(1)} %get-tuple-element.177), kind=kLoop, calls=%fused_computation.6.clone.1 | loop fusion | flops 47178240 | bytes 62976000 | tf_op jit(solution)/shard_map/while/body/eval_jaxpr/reduce_sum | solution.py:87
  449.6 23.8 %bitcast_divide_fusion.3 = f32[960,8,96]{0,2,1:T(8,128)} fusion(bf16[2048,8,96]{0,2,1:T(8,128)(2,1)S(1)} %bitcast.103, f32[8,960,2048]{2,1,0:T(8,128)} %get-tuple-element.176, f32[8,960]{1,0:T(8,128)S(1)} %get-tuple-element.177, f32[960,8]{0,1:T(8,128)S(1)} %bitcast.121), kind=kOutput, calls=%fused_computation.9.clone.1 | convolution fusion | flops 3067822080 | bytes 69070848 | tf_op jit(solution)/shard_map/while/body/eval_jaxpr/hrp,phd->rhd/dot_general | solution.py:89
  473.5 7.5 copy.168
  481.0 51.7 %dynamic_update_slice.16 = f32[2,960,768]{2,0,1:T(2,128)} dynamic-update-slice(f32[2,960,768]{2,0,1:T(2,128)} %get-tuple-element.190, f32[1,960,768]{2,0,1:T(1,128)S(1)} %copy.168, s32[]{:T(128)S(6)} %copy.176, s32[]{:T(128)} %constant.26.clone.1..sunk, s32[]{:T(128)} %constant.26.clone.1..sunk) | dynamic-update-slice | bytes 5898244 | tf_op jit(solution)/shard_map/while/body/jit(dynamic_update_index_in_dim)/dynamic_update_slice | solution.py:150
  532.8 1.5 constant_dynamic-slice_fusion.7
  534.2 1.6 copy.166
  535.9 2.1 constant_dynamic-slice_fusion.8
  538.0 3.0 copy.167
  541.0 2.1 constant_dynamic-slice_fusion.6
  543.1 3.0 copy.165
  546.0 24.0 %multiply_reduce_fusion.2 = (f32[8,960]{1,0:T(8,128)S(1)}, f32[8,960,2048]{2,1,0:T(8,128)}) fusion(bf16[960,8,96]{0,2,1:T(8,128)(2,1)} %bitcast.102, bf16[2048,8,96]{0,2,1:T(8,128)(2,1)} %bitcast.101), kind=kOutput, calls=%fused_computation.5.clone.1 | convolution fusion | flops 3051348480 | bytes 67565568 | tf_op jit(solution)/shard_map/while/body/eval_jaxpr/rhd,phd->hrp/dot_general | solution.py:82
  570.1 20.2 %fusion.75 = f32[8,960]{1,0:T(8,128)S(1)} fusion(f32[8,960,2048]{2,1,0:T(8,128)} %get-tuple-element.176, f32[8,960]{1,0:T(8,128)S(1)} %get-tuple-element.177), kind=kLoop, calls=%fused_computation.6.clone.1 | loop fusion | flops 47178240 | bytes 62976000 | tf_op jit(solution)/shard_map/while/body/eval_jaxpr/reduce_sum | solution.py:87
  590.3 23.8 %bitcast_divide_fusion.3 = f32[960,8,96]{0,2,1:T(8,128)} fusion(bf16[2048,8,96]{0,2,1:T(8,128)(2,1)S(1)} %bitcast.103, f32[8,960,2048]{2,1,0:T(8,128)} %get-tuple-element.176, f32[8,960]{1,0:T(8,128)S(1)} %get-tuple-element.177, f32[960,8]{0,1:T(8,128)S(1)} %bitcast.121), kind=kOutput, calls=%fused_computation.9.clone.1 | convolution fusion | flops 3067822080 | bytes 69070848 | tf_op jit(solution)/shard_map/while/body/eval_jaxpr/hrp,phd->rhd/dot_general | solution.py:89
  614.1 7.5 copy.168
  621.7 51.7 %dynamic_update_slice.16 = f32[2,960,768]{2,0,1:T(2,128)} dynamic-update-slice(f32[2,960,768]{2,0,1:T(2,128)} %get-tuple-element.190, f32[1,960,768]{2,0,1:T(1,128)S(1)} %copy.168, s32[]{:T(128)S(6)} %copy.176, s32[]{:T(128)} %constant.26.clone.1..sunk, s32[]{:T(128)} %constant.26.clone.1..sunk) | dynamic-update-slice | bytes 5898244 | tf_op jit(solution)/shard_map/while/body/jit(dynamic_update_index_in_dim)/dynamic_update_slice | solution.py:150
  673.4 0.9 copy.126
  674.3 2.1 reshape.329
  676.4 4.9 all-to-all-start.1
  681.3 0.9 copy.128
  682.2 1.5 reshape.331
  683.7 7.0 all_to_all.63
  690.7 7.3 all-to-all-start.3
  698.8 2.3 fusion.13
  701.2 4.7 copy-done.2
  705.9 2.7 fusion.15
  709.1 0.8 reduce.3
  709.9 1.5 reshape.330
  711.4 1.9 gather_fusion.1
  713.5 0.8 reduce.2
  714.3 1.5 reshape.332
  715.9 1.7 gather_fusion.2
  717.7 45.2 %all-to-all-done.3 = f32[2,960,768]{2,0,1:T(2,128)} async-done(((f32[2,960,768]{2,0,1:T(2,128)}), f32[2,960,768]{2,0,1:T(2,128)}, u32[]{:S(2)}, u32[]{:S(2)}) %all-to-all-start.3) | async-done | bytes 5898272 | tf_op jit(solution)/shard_map/all_to_all | solution.py:152
  762.9 3.2 copy.135
  766.1 3.1 copy.142
  769.1 9.0 reshape.327
  778.2 5.9 gather_fusion.3
  784.0 2.6 copy.138
  786.7 9.2 fusion.31
  795.9 9.3 fusion.57
  805.9 249.9 %reduce-scatter.2.cloned.1.call-done = f32[640,768]{1,0:T(8,128)} async-done(((f32[640,6144]{1,0:T(8,128)}), f32[640,768]{1,0:T(8,128)}) %reduce-scatter.2.cloned.1.call-update) | async-done | bytes 1966096 | tf_op jit(solution)/shard_map/reduce_scatter | solution.py:169
  1055.8 2.7 add_convert_fusion
  (99 shorter events, 6.3 us)
Async XLA Ops:
  6.5 1.5 copy-start.24
  6.5 1.6 copy-start.21
  6.5 1.8 copy-start.19
  6.5 2.0 copy-start.18
  6.5 120.6 %all-gather.3.cloned.1.call-start = ((), (), s32[]{:S(2)}) async-start(), calls=%async_computation.5 | async-start | bytes 8847360 | tf_op jit(solution)/shard_map/all_gather | solution.py:125
  7.3 293.0 %all-gather.5.cloned.1.call-start = ((), (), s32[]{:S(2)}) async-start(), calls=%async_computation.6 | async-start | bytes 35389440 | tf_op jit(solution)/shard_map/all_gather | solution.py:129
  9.3 0.7 copy-start.15
  10.2 330.6 %copy-start.7 = (f32[640,12]{0,1:T(8,128)}, f32[640,12]{0,1:T(8,128)S(1)}, u32[]{:S(2)}) copy-start(f32[640,12]{0,1:T(8,128)S(1)} %get-tuple-element.121) | copy-start | bytes 92164
  10.2 330.6 %copy-start.9 = (f32[640,12]{0,1:T(8,128)}, f32[640,12]{0,1:T(8,128)S(1)}, u32[]{:S(2)}) copy-start(f32[640,12]{0,1:T(8,128)S(1)} %get-tuple-element.122) | copy-start | bytes 92164
  127.1 5.5 copy-start.1
  131.6 168.6 %copy-start.22 = (f32[6144]{0:T(1024)S(1)}, f32[6144]{0:T(1024)}, u32[]{:S(2)}) copy-start(f32[6144]{0:T(1024)} %param.16) | copy-start | bytes 73732
  131.6 168.6 %copy-start.23 = (f32[6144]{0:T(1024)S(1)}, f32[6144]{0:T(1024)}, u32[]{:S(2)}) copy-start(f32[6144]{0:T(1024)} %param.15) | copy-start | bytes 73732
  341.0 7.7 copy-start.5
  351.9 38.4 %all-to-all-start = ((bf16[8,240,768]{2,1,0:T(8,128)(2,1)}), bf16[8,240,768]{2,1,0:T(8,128)(2,1)S(1)}, u32[]{:S(2)}, u32[]{:S(2)}) async-start(bf16[8,240,768]{2,1,0:T(8,128)(2,1)} %broadcast_select_fusion), calls=%async_computation | async-start | bytes 5898240 | tf_op jit(solution)/shard_map/all_to_all | solution.py:149
  429.4 20.2 %copy-start = (bf16[1,2048,768]{1,2,0:T(8,128)(2,1)S(1)}, bf16[1,2048,768]{1,2,0:T(8,128)(2,1)}, u32[]{:S(2)}) copy-start(bf16[1,2048,768]{1,2,0:T(8,128)(2,1)} %copy.165) | copy-start | bytes 9437188 | tf_op jit(solution)/shard_map/while
  570.0 20.2 %copy-start = (bf16[1,2048,768]{1,2,0:T(8,128)(2,1)S(1)}, bf16[1,2048,768]{1,2,0:T(8,128)(2,1)}, u32[]{:S(2)}) copy-start(bf16[1,2048,768]{1,2,0:T(8,128)(2,1)} %copy.165) | copy-start | bytes 9437188 | tf_op jit(solution)/shard_map/while
  676.4 7.3 all-to-all-start.1
  683.7 7.0 copy-start.11
  690.7 7.5 copy-start.16
  690.7 7.6 copy-start.17
  690.7 7.6 copy-start.14
  690.7 7.9 copy-start.3
  690.7 8.0 copy-start.8
  690.7 8.0 copy-start.10
  690.7 8.1 copy-start.6
  690.7 72.1 %all-to-all-start.3 = ((f32[2,960,768]{2,0,1:T(2,128)}), f32[2,960,768]{2,0,1:T(2,128)}, u32[]{:S(2)}, u32[]{:S(2)}) async-start(f32[2,960,768]{2,0,1:T(2,128)} %get-tuple-element.46), calls=%async_computation.3 | async-start | bytes 11796480 | tf_op jit(solution)/shard_map/all_to_all | solution.py:152
  698.0 357.8 %reduce-scatter.2.cloned.1.call-start = ((), (), s32[]{:S(2)}) async-start(), calls=%async_computation.7 | async-start | bytes 17694720 | tf_op jit(solution)/shard_map/reduce_scatter | solution.py:169
  701.2 4.7 copy-start.2
  705.9 3.2 copy-start.12
  708.5 4.9 copy-start.13
  784.0 11.8 %slice-start = ((s8[9437184]{0:T(1024)(128)(4,1)}), s8[1048576]{0:T(1024)(128)(4,1)S(1)}, s32[]{:S(2)}) async-start(s8[9437184]{0:T(1024)(128)(4,1)} %bitcast.107), calls=%async_computation.8 | async-start | bytes 2097152
  786.6 9.2 slice-start.1
  786.6 9.2 slice-start.2
  805.2 0.7 copy-start.20
  805.2 250.6 %copy-start.4 = (bf16[640,768]{1,0:T(8,128)(2,1)S(1)}, bf16[640,768]{1,0:T(8,128)(2,1)}, u32[]{:S(2)}) copy-start(bf16[640,768]{1,0:T(8,128)(2,1)} %param.14) | copy-start | bytes 2949124
Sparse Core Ops, SparseCore 0:
  9.5 117.5 all-gather.2
  128.7 171.5 all-gather.4
  805.4 250.3 reduce-scatter.1
where the time goes:
time: 1090 us; the launch traced here: 1070 us
  waiting for transfers between devices  612 us (56%)
  local copies, waits for them, and re-layouts  209 us (19%)
  matrix products  145 us (13%)
  other arithmetic  60 us (6%)
  starting transfers between devices  17.8 us (2%)
  between operations  14.1 us (1%)
    reduce_scatter x1, waiting for transfers between devices, on_device(): lax.psum_scatter(partial_out, 'head', scatter_dimension=1, tiled=True)  250 us
    all_gather x1, waiting for transfers between devices, on_device(): lax.all_gather(qkv_weight, 'tok', axis=0, tiled=True)  165 us
    dynamic_update_slice x6, local copies, waits for them, and re-layouts, on_device(): lax.map(prefix_slot, (incoming, prefix_keys, prefix_values))  119 us
    all_gather x1, waiting for transfers between devices, on_device(): full_rows = lax.all_gather(hidden_states, 'head', axis=1, tiled=True)  117 us
    dot_general x2, matrix products, prefix_slot(): jnp.einsum('rhd,phd->hrp', query_heads, key_heads, preferred_element_type...  48 us
    dot_general x2, matrix products, prefix_slot(): jnp.einsum('hrp,phd->rhd', weights.astype(jnp.bfloat16), value_heads, pre...  47.7 us
    all_to_all x1, waiting for transfers between devices, on_device(): lax.all_to_all(pre_all, 'tok', split_axis=1, concat_axis=0, tiled=True)  45.2 us
    reduce_sum x2, other arithmetic, prefix_slot(): row_mass = jnp.sum(weights, axis=-1)  40.4 us
  transfers between devices with their start and end apart: 6, of which 5 were waited for; matrix products, arithmetic and copies ran while one was open for 2% of the time, Pallas kernels for 0%

commit v1 on v0

v1 whole, which is shorter than its diff:
```python
import functools
import math

import jax
import jax.numpy as jnp
from jax import lax
from jax.experimental import pallas as pl
from jax.experimental.pallas import tpu as pltpu
from jax.sharding import PartitionSpec as P

HS = 96
GROUP_HEADS = 4
GW = GROUP_HEADS * HS
PACK = 128
F32 = jnp.float32
BF16 = jnp.bfloat16
VMEM_LIMIT = 56 * 1024 * 1024
SCALE = 1.0 / math.sqrt(HS)
LOG2E = math.log2(math.e)


def windows():
    found = []
    for k in range(GROUP_HEADS):
        first = k * HS // 128 * 128
        last = -(-(k * HS + HS) // 128) * 128
        found.append((first, last - first))
    return found


def head_mask(k, first, shape):
    lane = lax.broadcasted_iota(jnp.int32, shape, 1) + first
    return (lane >= k * HS) & (lane < (k + 1) * HS)


def params():
    return pltpu.CompilerParams(vmem_limit_bytes=VMEM_LIMIT)


def layer_norm(values_in, gain, shift):
    widened = values_in.astype(F32)
    center = jnp.mean(widened, axis=-1, keepdims=True)
    spread = jnp.mean(jnp.square(widened - center), axis=-1, keepdims=True)
    return ((widened - center) * lax.rsqrt(spread + 1e-05) * gain + shift).astype(BF16)


def shard_layout(lengths, ordering, row_count):
    group_count = lengths.shape[0]
    labels = jnp.arange(group_count, dtype=jnp.int32)
    chosen = (ordering[:, None] == labels[None, :]).astype(jnp.int32)
    ranking = jnp.sum(labels[:, None] * chosen, axis=0)
    earlier = (ranking[None, :] < ranking[:, None]).astype(jnp.int32)
    starts = jnp.sum(earlier * lengths[None, :], axis=1)
    places = jnp.arange(row_count, dtype=jnp.int32)
    member = (
        (places[:, None] >= starts[None, :]) & (places[:, None] < (starts + lengths)[None, :])
    ).astype(jnp.int32)
    row_start = jnp.sum(member * starts[None, :], axis=1)
    return starts, row_start, places - row_start


def rotary_tables(positions):
    rot = HS // 4
    half = rot // 2
    inverse = 10000.0 ** (-(jnp.arange(half, dtype=F32) * 2.0) / rot)
    angles = positions.astype(F32)[:, None] * inverse[None, :]
    cosine, sine = jnp.cos(angles), jnp.sin(angles)
    rows = positions.shape[0]
    rest = jnp.zeros((rows, HS - rot), F32)
    none = jnp.zeros((rows, half), F32)
    straight = jnp.concatenate([cosine, cosine, rest + 1.0], axis=1)
    upper = jnp.concatenate([-sine, none, rest], axis=1)
    lower = jnp.concatenate([none, sine, rest], axis=1)
    return [jnp.tile(table, (1, GROUP_HEADS)) for table in (straight, upper, lower)]


def qkv_kernel(pieces, order, normed, *refs):
    weights = refs[:pieces]
    bias, straight, upper, lower, q_out, k_out, v_out, total = refs[pieces:]
    step = pl.program_id(0)
    depth = weights[0].shape[0]
    summed = None
    for j in range(pieces):
        columns = pl.ds(pl.multiple_of(order[j] * depth, 128), depth)
        part = jnp.dot(normed[:, columns], weights[j][...], preferred_element_type=F32)
        summed = part if summed is None else summed + part
    total[step] = summed + bias[...]

    @pl.when(step == 2)
    def _():
        tile = 64

        def body(i, carry):
            rows = pl.ds(pl.multiple_of(i * tile, tile), tile)
            wide = jnp.concatenate([total[n, rows, :] for n in range(3)], axis=1)

            def part(c):
                result = None
                for k in range(GROUP_HEADS):
                    first = 192 * k + HS * c
                    cut = wide[:, first : first + GW]
                    if result is None:
                        result = cut
                    else:
                        result = jnp.where(head_mask(k, 0, cut.shape), cut, result)
                return result

            def turn(x):
                return (
                    x * straight[rows, :]
                    + pltpu.roll(x, GW - HS // 8, 1) * upper[rows, :]
                    + pltpu.roll(x, HS // 8, 1) * lower[rows, :]
                )

            q_out[rows, :] = turn(part(0)).astype(BF16)
            k_out[rows, :] = turn(part(1)).astype(BF16)
            v_out[rows, :] = part(2).astype(BF16)
            return carry

        lax.fori_loop(0, total.shape[1] // tile, body, 0)


def project(normed, weights, order, bias, tables):
    rows, features = normed.shape
    pieces = len(weights)
    depth, columns = weights[0].shape
    out = jax.ShapeDtypeStruct((rows, GW), BF16)
    whole = lambda n, order: (0, 0)
    tile = lambda n, order: (0, n)
    return pl.pallas_call(
        functools.partial(qkv_kernel, pieces),
        out_shape=(out, out, out),
        grid_spec=pltpu.PrefetchScalarGridSpec(
            num_scalar_prefetch=1,
            grid=(columns // GW,),
            in_specs=[pl.BlockSpec((rows, features), whole)]
            + [pl.BlockSpec((depth, GW), tile)] * pieces
            + [pl.BlockSpec((1, GW), tile)]
            + [pl.BlockSpec((rows, GW), whole)] * 3,
            out_specs=[pl.BlockSpec((rows, GW), whole)] * 3,
            scratch_shapes=[pltpu.VMEM((columns // GW, rows, GW), F32)],
        ),
        compiler_params=params(),
        cost_estimate=pl.CostEstimate(
            flops=2 * rows * features * columns,
            bytes_accessed=2 * features * (rows + columns) + 9 * rows * GW * 2,
            transcendentals=0,
        ),
        name="project",
    )(order, normed, *weights, bias, *tables)


def prefix_kernel(blocks, starts, lengths, *refs):
    queries = refs[:blocks]
    k_own, k_other, v_own, v_other = refs[blocks : blocks + 4]
    outs = refs[blocks + 4 : 2 * blocks + 4]
    totals = refs[2 * blocks + 4]
    slot = pl.program_id(0)
    slots = pl.num_programs(0)
    rows = queries[0].shape[0]
    length = k_own.shape[1]

    @pl.when(slot == 0)
    def _():
        totals[...] = jnp.zeros_like(totals)

    begin, size, offset = [], [], []
    count = 0
    for b in range(blocks):
        begin.append(starts[slot * blocks + b])
        size.append(lengths[slot * blocks + b])
        offset.append(count)
        count = count + size[b]

    def serve(keys, values):
        def tile(base, height):
            down = lax.broadcasted_iota(jnp.int32, (height, 1), 0) + base
            across = lax.broadcasted_iota(jnp.int32, (1, height), 1) + base

            def sources(place, b):
                within = place - offset[b]
                return jnp.where((within >= 0) & (within < size[b]), within + begin[b], -1)

            picked = None
            for b in range(blocks):
                spread = lax.broadcasted_iota(jnp.int32, (height, rows), 1)
                one_hot = jnp.where(spread == sources(down, b), 1.0, 0.0).astype(BF16)
                part = jnp.dot(one_hot, queries[b][...], preferred_element_type=F32)
                picked = part if picked is None else picked + part
            picked = picked.astype(BF16)
            merged = [jnp.zeros((height, 128), F32) for _ in range(GW // 128)]
            extra = jnp.zeros((height, PACK), F32)
            place = lax.broadcasted_iota(jnp.int32, (height, PACK), 1)
            for k, (first, width) in enumerate(windows()):
                lanes = slice(first, first + width)
                mask = head_mask(k, first, (height, width))
                query = jnp.where(mask, picked[:, lanes], jnp.zeros((), BF16))
                scores = lax.dot_general(
                    query,
                    keys[0, :, lanes],
                    (((1,), (1,)), ((), ())),
                    preferred_element_type=F32,
                )
                peak = jnp.max(scores, axis=1, keepdims=True)
                weights = jnp.exp2((scores - peak) * (SCALE * LOG2E))
                mass = jnp.sum(weights, axis=1, keepdims=True)
                blended = jnp.dot(
                    weights.astype(BF16), values[0, :, lanes], preferred_element_type=F32
                )
                blended = blended * (1.0 / mass)
                for w in range(width // 128):
                    at = first // 128 + w
                    cut = slice(w * 128, w * 128 + 128)
                    merged[at] = jnp.where(mask[:, cut], blended[:, cut], merged[at])
                level = peak * SCALE + jnp.log(mass)
                high = level.astype(BF16).astype(F32)
                middle = (level - high).astype(BF16).astype(F32)
                low = level - high - middle
                for n, term in enumerate((high, middle, low)):
                    extra = jnp.where(place == 3 * k + n, term, extra)
            packed = jnp.concatenate(merged + [extra], axis=1).astype(BF16)
            for b in range(blocks):
                spread = lax.broadcasted_iota(jnp.int32, (rows, height), 0)
                one_hot = jnp.where(spread == sources(across, b), 1.0, 0.0).astype(BF16)
                totals[b] += jnp.dot(one_hot, packed, preferred_element_type=F32)

        large = 256
        small = 128
        full = lax.div(count, large)
        rest = count - full * large

        def body(j, carry):
            tile(j * large, large)
            return carry

        lax.fori_loop(0, full + jnp.where(rest > small, 1, 0), body, 0)

        @pl.when((rest > 0) & (rest <= small))
        def _():
            tile(full * large, small)

    half = slots // 2

    @pl.when(slot < half)
    def _():
        serve(k_own, v_own)

    @pl.when(slot >= half)
    def _():
        serve(k_other, v_other)

    @pl.when(slot == slots - 1)
    def _():
        for b in range(blocks):
            outs[b][...] = totals[b].astype(BF16)


def prefix_attention(group, queries, cache, starts, lengths):
    blocks = len(queries)
    rows = queries[0].shape[0]
    held, length, _ = cache[0].shape
    width = GW + PACK
    whole = lambda s, starts, lengths: (0, 0)
    own = lambda s, starts, lengths: (jnp.minimum(s, held - 1), 0, group)
    other = lambda s, starts, lengths: (jnp.maximum(s - held, 0), 0, group)
    block = (1, length, GW)
    return pl.pallas_call(
        functools.partial(prefix_kernel, blocks),
        out_shape=[jax.ShapeDtypeStruct((rows, width), BF16)] * blocks,
        grid_spec=pltpu.PrefetchScalarGridSpec(
            num_scalar_prefetch=2,
            grid=(2 * held,),
            in_specs=[pl.BlockSpec((rows, GW), whole)] * blocks
            + [
                pl.BlockSpec(block, own),
                pl.BlockSpec(block, other),
                pl.BlockSpec(block, own),
                pl.BlockSpec(block, other),
            ],
            out_specs=[pl.BlockSpec((rows, width), whole)] * blocks,
            scratch_shapes=[pltpu.VMEM((blocks, rows, width), F32)],
        ),
        compiler_params=params(),
        cost_estimate=pl.CostEstimate(
            flops=4 * rows * length * GROUP_HEADS * 256,
            bytes_accessed=2 * 2 * held * length * GW * 2,
            transcendentals=rows * length * GROUP_HEADS,
        ),
        name="prefix",
    )(starts, lengths, *queries, cache[0], cache[1], cache[2], cache[3])


def suffix_kernel(row_start, queries, keys, values, out, levels):
    rows = queries.shape[0]
    tile = 128
    for i in range(rows // tile):
        at = slice(i * tile, (i + 1) * tile)
        wide = (i + 1) * tile
        row = lax.broadcasted_iota(jnp.int32, (tile, wide), 0) + i * tile
        column = lax.broadcasted_iota(jnp.int32, (tile, wide), 1)
        allowed = (column <= row) & (column >= row_start[at, :])
        merged = [jnp.zeros((tile, 128), F32) for _ in range(GW // 128)]
        level_row = jnp.zeros((tile, PACK), F32)
        place = lax.broadcasted_iota(jnp.int32, (tile, PACK), 1)
        for k, (first, width) in enumerate(windows()):
            lanes = slice(first, first + width)
            mask = head_mask(k, first, (tile, width))
            query = jnp.where(mask, queries[at, lanes], jnp.zeros((), BF16))
            scores = lax.dot_general(
                query,
                keys[:wide, lanes],
                (((1,), (1,)), ((), ())),
                preferred_element_type=F32,
            )
            scores = jnp.where(allowed, scores, -jnp.inf)
            peak = jnp.max(scores, axis=1, keepdims=True)
            weights = jnp.exp2((scores - peak) * (SCALE * LOG2E))
            mass = jnp.sum(weights, axis=1, keepdims=True)
            blended = jnp.dot(
                weights.astype(BF16), values[:wide, lanes], preferred_element_type=F32
            )
            blended = blended * (1.0 / mass)
            for w in range(width // 128):
                spot = first // 128 + w
                cut = slice(w * 128, w * 128 + 128)
                merged[spot] = jnp.where(mask[:, cut], blended[:, cut], merged[spot])
            level_row = jnp.where(place == k, peak * SCALE + jnp.log(mass), level_row)
        out[at, :] = jnp.concatenate(merged, axis=1)
        levels[at, :] = level_row


def suffix_attention(row_start, queries, keys, values):
    rows = queries.shape[0]
    return pl.pallas_call(
        suffix_kernel,
        out_shape=(
            jax.ShapeDtypeStruct((rows, GW), F32),
            jax.ShapeDtypeStruct((rows, PACK), F32),
        ),
        compiler_params=params(),
        cost_estimate=pl.CostEstimate(
            flops=4 * rows * rows * GROUP_HEADS * 256,
            bytes_accessed=rows * GW * 10,
            transcendentals=rows * rows * GROUP_HEADS,
        ),
        name="suffix",
    )(row_start, queries, keys, values)


def merge_kernel(blocks, *refs):
    parts = refs[:blocks]
    suffix, levels, out = refs[blocks:]
    rows = suffix.shape[0]
    tile = 128
    for i in range(rows // tile):
        at = slice(i * tile, (i + 1) * tile)
        prefix = parts[0][at, :].astype(F32)
        for b in range(1, blocks):
            prefix = prefix + parts[b][at, :].astype(F32)
        share_pre = jnp.zeros((tile, GW), F32)
        share_suf = jnp.zeros((tile, GW), F32)
        for k in range(GROUP_HEADS):
            lane = GW + 3 * k
            pre = (
                prefix[:, lane : lane + 1]
                + prefix[:, lane + 1 : lane + 2]
                + prefix[:, lane + 2 : lane + 3]
            )
            suf = levels[at, k : k + 1]
            top = jnp.maximum(pre, suf)
            pre = jnp.exp(pre - top)
            suf = jnp.exp(suf - top)
            whole = 1.0 / (pre + suf)
            mask = head_mask(k, 0, (tile, GW))
            share_pre = jnp.where(mask, pre * whole, share_pre)
            share_suf = jnp.where(mask, suf * whole, share_suf)
        out[at, :] = (share_pre * prefix[:, :GW] + share_suf * suffix[at, :]).astype(BF16)


def merge(parts, suffix, levels):
    rows = suffix.shape[0]
    return pl.pallas_call(
        functools.partial(merge_kernel, len(parts)),
        out_shape=jax.ShapeDtypeStruct((rows, GW), BF16),
        compiler_params=params(),
        cost_estimate=pl.CostEstimate(
            flops=rows * GW * 8, bytes_accessed=rows * GW * 10, transcendentals=rows * 8
        ),
        name="merge",
    )(*parts, suffix, levels)


def on_device(
    hidden_states,
    norm_gain,
    norm_bias,
    qkv_weight,
    qkv_bias,
    dense_weight,
    dense_bias,
    prefix_keys,
    prefix_values,
    suffix_len,
    request_order,
    group_slot,
):
    rows, share = hidden_states.shape
    held, prefix_length, local_width = prefix_keys.shape
    groups_local = local_width // GW
    tok_size = lax.axis_size("tok")
    head_size = lax.axis_size("head")
    chips = tok_size // 2
    lines = head_size // 2
    group_count = held * tok_size
    tok = lax.axis_index("tok")
    head = lax.axis_index("head")
    core, chip = tok % 2, tok // 2
    side, line = head % 2, head // 2

    def to_core(x):
        return lax.ppermute(x, "tok", [(t, t ^ 1) for t in range(tok_size)])

    def to_chip(x, shift):
        return lax.ppermute(
            x,
            "tok",
            [(t, (t // 2 + shift) % chips * 2 + t % 2) for t in range(tok_size)],
        )

    def to_side(x):
        return lax.ppermute(x, "head", [(h, h ^ 1) for h in range(head_size)])

    columns = 3 * GW
    order = [tok, tok ^ 1]
    for shift in range(1, chips):
        source = (chip + chips - shift) % chips * 2 + core
        order += [source, source ^ 1]
    order = jnp.stack(order).astype(jnp.int32)
    gathered = []
    for g in range(groups_local):
        mine = qkv_weight[:, g * columns : (g + 1) * columns]
        pieces = [mine, to_core(mine)]
        for shift in range(1, chips):
            arrived = to_chip(mine, shift)
            pieces += [arrived, to_core(arrived)]
        gathered.append(pieces)
    full_rows = lax.all_gather(hidden_states, "head", axis=1, tiled=True)
    cache = [prefix_keys, to_core(prefix_keys), prefix_values, to_core(prefix_values)]

    lengths = suffix_len[0]
    starts, row_start, within = shard_layout(lengths, request_order[0], rows)
    labels = jnp.arange(group_count, dtype=jnp.int32)
    slot_match = (group_slot[:, None] == labels[None, :]).astype(jnp.int32)
    spans = jnp.stack(
        [
            jnp.sum(starts[:, None] * slot_match, axis=0),
            jnp.sum(lengths[:, None] * slot_match, axis=0),
        ]
    )
    all_spans = [spans] + [to_chip(spans, shift) for shift in range(1, chips)]
    served = jnp.stack(
        [
            jnp.concatenate(
                [
                    lax.dynamic_slice(one, (0, tok * held), (2, held)),
                    lax.dynamic_slice(one, (0, (tok ^ 1) * held), (2, held)),
                ],
                axis=1,
            )
            for one in all_spans
        ],
        axis=2,
    )
    span_start = served[0].reshape(-1)
    span_length = served[1].reshape(-1)
    tables = rotary_tables(prefix_length + within)
    bias = qkv_bias.astype(F32)[None, :]

    def side_columns(which):
        return [
            lax.dynamic_slice(
                dense_weight, (0, (2 * a + which) * share), (dense_weight.shape[0], share)
            )
            for a in range(lines)
        ]

    half = lines // 2
    outgoing = lax.dynamic_slice(
        jnp.concatenate(side_columns(1 - side), axis=1),
        (0, core * half * share),
        (dense_weight.shape[0], half * share),
    )
    landed = to_side(outgoing)
    crossed = to_core(landed)
    received = jnp.where(
        core == 0,
        jnp.concatenate([landed, crossed], axis=1),
        jnp.concatenate([crossed, landed], axis=1),
    )
    dense_both = jnp.concatenate(
        [jnp.concatenate(side_columns(side), axis=1), received], axis=0
    )

    normed = layer_norm(full_rows, norm_gain, norm_bias)
    attention_own, attention_side = [], []
    for g in range(groups_local):
        queries, keys, values = project(
            normed, gathered[g], order, bias[:, g * columns : (g + 1) * columns], tables
        )
        asked = [queries] + [to_chip(queries, shift) for shift in range(1, chips)]
        answers = prefix_attention(g, asked, cache, span_start, span_length)
        parts = [answers[0]] + [to_chip(answers[s], chips - s) for s in range(1, chips)]
        suffix, levels = suffix_attention(row_start[:, None], queries, keys, values)
        attention = merge(parts, suffix, levels)
        attention_own.append(attention)
        attention_side.append(to_side(attention))
    attention = jnp.concatenate(attention_own + attention_side, axis=1)
    partial = jnp.dot(attention, dense_both, preferred_element_type=F32)

    def chunk(place):
        place = jnp.clip(place, 0, lines - 1)
        return lax.dynamic_slice(partial, (0, place * share), (rows, share))

    upward = downward = None
    last = lines - 1
    for step in range(last):
        up = chunk(last + line - step)
        down = chunk(line - last + step)
        if upward is not None:
            up = up + upward.astype(F32)
            down = down + downward.astype(F32)
        up_pairs = [(h, h + 2) for h in range(head_size) if h // 2 <= step and h // 2 < last]
        down_pairs = [(h, h - 2) for h in range(head_size) if last - h // 2 <= step and h // 2 > 0]
        upward = lax.ppermute(up.astype(BF16), "head", up_pairs)
        downward = lax.ppermute(down.astype(BF16), "head", down_pairs)
    summed = chunk(line) + upward.astype(F32) + downward.astype(F32)
    return (hidden_states.astype(F32) + dense_bias.astype(F32) + summed).astype(BF16)


def solution(mesh):
    placed = (
        P("tok", "head"),
        P(),
        P(),
        P("tok", "head"),
        P("head"),
        P("head", None),
        P("head"),
        P("tok", None, "head"),
        P("tok", None, "head"),
        P("tok", None),
        P("tok", None),
        P(),
    )
    return jax.shard_map(
        on_device, mesh=mesh, in_specs=placed, out_specs=P("tok", "head"), check_vma=False
    )
```

time: 1090 us -> 490 us (0.45); the launches traced: 1070 us -> 481 us
  waiting for transfers between devices: 612 us -> 233 us
  local copies, waits for them, and re-layouts: 209 us -> 27.1 us
  Pallas kernels: 0 us -> 142 us
  matrix products: 145 us -> 9.04 us
  other arithmetic: 60 us -> 35.5 us
    reduce_scatter x1 -> x0, waiting for transfers between devices: 250 us -> none  [on_device(): lax.psum_scatter(partial_out, 'head', scatter_dimension=1, tiled=True)]
    ppermute x0 -> x23, waiting for transfers between devices: none -> 232 us  [the longest x7 142 us: to_chip(): lax.ppermute(x, 'tok', [(t, (t // 2 + shift) % chips * 2 + t % 2) for t i...]
    all_gather x1 -> x0, waiting for transfers between devices: 165 us -> none  [on_device(): lax.all_gather(qkv_weight, 'tok', axis=0, tiled=True)]
    pallas_call x0 -> x8, Pallas kernels: none -> 142 us  [the longest x2 60.1 us: prefix_attention(): pl.pallas_call(functools.partial(prefix_kernel, blocks), out_shape=[jax.S...]
    dot_general x8 -> x1, matrix products: 145 us -> 9.04 us  [on_device(): partial = jnp.dot(attention, dense_both, preferred_element_type=F32)]
    dynamic_update_slice x6 -> x0, local copies, waits for them, and re-layouts: 119 us -> none  [on_device(): lax.map(prefix_slot, (incoming, prefix_keys, prefix_values))]
    all_gather x1, waiting for transfers between devices: 117 us -> 0.01 us  [on_device(): full_rows = lax.all_gather(hidden_states, 'head', axis=1, tiled=True)]
    all_to_all x3 -> x0, waiting for transfers between devices: 78.3 us -> none  [the longest x1 45.2 us: on_device(): lax.all_to_all(pre_all, 'tok', split_axis=1, concat_axis=0, tiled=True)]
  transfers between devices with their start and end apart: 6 -> 24, of which waited for: 5 -> 7; matrix products, arithmetic and copies ran while one was open for 2% -> 10% of each run, Pallas kernels for 0% -> 30%
where the time goes in v1:
time: 490 us; the launch traced here: 481 us
  waiting for transfers between devices  233 us (48%)
  Pallas kernels  142 us (29%)
  other arithmetic  35.5 us (7%)
  local copies, waits for them, and re-layouts  27.1 us (6%)
  starting transfers between devices  20.5 us (4%)
  between operations  14 us (3%)
  matrix products  9.04 us (2%)
    ppermute x7, waiting for transfers between devices, to_chip(): lax.ppermute(x, 'tok', [(t, (t // 2 + shift) % chips * 2 + t % 2) for t i...  142 us
    pallas_call x2, Pallas kernels, prefix_attention(): pl.pallas_call(functools.partial(prefix_kernel, blocks), out_shape=[jax.S...  60.1 us
    pallas_call x2, Pallas kernels, project(): pl.pallas_call(functools.partial(qkv_kernel, pieces), out_shape=(out, out...  50.8 us
    ppermute x3, waiting for transfers between devices, on_device(): upward = lax.ppermute(up.astype(BF16), 'head', up_pairs)  44.2 us
    ppermute x3, waiting for transfers between devices, on_device(): downward = lax.ppermute(down.astype(BF16), 'head', down_pairs)  37.1 us
    pallas_call x2, Pallas kernels, merge(): pl.pallas_call(functools.partial(merge_kernel, len(parts)), out_shape=jax...  16.1 us
    pallas_call x2, Pallas kernels, suffix_attention(): pl.pallas_call(suffix_kernel, out_shape=(jax.ShapeDtypeStruct((rows, GW),...  15.3 us
  transfers between devices with their start and end apart: 24, of which 7 were waited for; matrix products, arithmetic and copies ran while one was open for 10% of the time, Pallas kernels for 30%

profile of v1, /device:TPU:14, one launch (start us, length us, event | category | flops | bytes accessed | tf_op | source)
XLA Modules:
  0.0 481.2 jit_solution(8111134513247345130)
XLA Ops:
  6.5 0.7 all-gather.2.cloned.1.call-update
  7.3 6.6 %fusion.31 = (bf16[1536,1152]{1,0:T(8,128)(2,1)}, bf16[1536,1152]{1,0:T(8,128)(2,1)}) fusion(bf16[1536,2304]{1,0:T(8,128)(2,1)} %param.15), kind=kLoop, calls=%fused_computation.83 | loop fusion | bytes 14155776 | tf_op jit(solution)/shard_map/slice | solution.py:441
  13.9 0.5 collective-permute-start.2
  14.4 6.3 %constant_dynamic-slice_fusion.7 = (bf16[768,768]{1,0:T(8,128)(2,1)}, bf16[768,768]{1,0:T(8,128)(2,1)S(1)}, bf16[768,768]{1,0:T(8,128)(2,1)S(1)}, bf16[768,768]{...) fusion(bf16[768,6144]{1,0:T(8,128)(2,1)} %param.17, ...), kind=kLoop, calls=%fused_computation.57 | loop fusion | bytes 18874400 | tf_op jit(solution)/shard_map/dynamic_slice | solution.py:481
  20.6 1.6 fusion.18
  22.3 0.6 collective-permute-start.15
  22.9 1.9 collective-permute-start.9
  24.8 0.2 select_reduce_fusion.3
  25.1 0.2 collective-permute-start
  25.5 0.2 multiply_sine_fusion
  25.9 142.4 %collective-permute-done = s32[2,8]{1,0:T(2,128)S(1)} collective-permute-done((s32[2,8]{1,0:T(2,128)S(1)}, s32[2,8]{1,0:T(2,128)S(1)}, u32[]{:S(2)}, u32[]{:S(2)}) %collective-permute-start) | collective-permute-done | bytes 96 | tf_op jit(solution)/shard_map/ppermute | solution.py:424
  168.3 0.5 collective-permute-start.6
  168.8 0.1 maximum_maximum_fusion.2
  169.0 1.3 copy.27.refs_5_
  170.4 1.3 copy.28.refs_6_
  171.7 1.4 copy.29.refs_7_
  173.1 0.7 pad_add_fusion.2.order
  173.8 0.6 fusion.32
  174.6 0.1 copy.25
  174.7 0.7 reshape_squeeze.6.starts
  175.5 0.6 reshape_squeeze.7.lengths
  176.1 4.5 convert_reduce_fusion
  180.6 0.6 collective-permute-start.8
  181.3 0.3 copy-done
  181.6 2.2 fusion.2
  183.8 7.8 %fusion.5.normed = bf16[640,6144]{1,0:T(8,128)(2,1)} fusion(bf16[640,6144]{1,0:T(8,128)(2,1)S(1)} %copy-done, f32[6144]{0:T(1024)S(1)} %copy-done.8, f32[6144]{0:T(1024)S(1)} %copy-done.9, f32[640]{0:T(1024)S(1)} %add_rsqrt_fusion, f32[640]{0:T(1024)S(1)} %broadcast_multiply_fusion), kind=kLoop, calls=%fused_computation.7 | loop fusion | flops 23592960 | bytes 15782912 | tf_op jit(solution)/shard_map/convert_element_type | solution.py:44
  191.6 1.3 collective-permute-done.3.refs_3_
  192.9 0.1 collective-permute-start.16
  193.0 25.5 %project.2 = (bf16[640,384]{1,0:T(8,128)(2,1)}, bf16[640,384]{1,0:T(8,128)(2,1)}, bf16[640,384]{1,0:T(8,128)(2,1)}) custom-call(s32[4]{0:T(128)} %pad_add_fusion.2.order, bf16[640,6144]{1,0:T(8,128)(2,1)} %fusion.5.normed, bf16[1536,1152]{1,0:T(8,128)(2,1)} %get-tuple-element.47.refs_0_, bf16[1536,1152]{1,0:T(8,128)(2,1)} %collective-permute-done.1.refs_1_, ...), custom_call_target="tpu_custom_call" | custom-call | flops 9059696640 | bytes 26443776 | tf_op jit(solution)/shard_map/project/pallas_call | solution.py:130
  218.5 0.6 collective-permute-start.4
  219.1 25.3 %project.3 = (bf16[640,384]{1,0:T(8,128)(2,1)}, bf16[640,384]{1,0:T(8,128)(2,1)}, bf16[640,384]{1,0:T(8,128)(2,1)}) custom-call(s32[4]{0:T(128)} %pad_add_fusion.2.order, bf16[640,6144]{1,0:T(8,128)(2,1)} %fusion.5.normed, bf16[1536,1152]{1,0:T(8,128)(2,1)} %get-tuple-element.48.refs_0_, bf16[1536,1152]{1,0:T(8,128)(2,1)} %collective-permute-done.8.refs_1_, ...), custom_call_target="tpu_custom_call" | custom-call | flops 9059696640 | bytes 26443776 | tf_op jit(solution)/shard_map/project/pallas_call | solution.py:130
  244.4 1.5 collective-permute-start.11
  245.9 0.8 copy-done.6
  246.7 35.0 %prefix.2 = (bf16[640,512]{1,0:T(8,128)(2,1)}, bf16[640,512]{1,0:T(8,128)(2,1)}) custom-call(s32[8]{0:T(128)} %reshape_squeeze.6.starts, s32[8]{0:T(128)} %reshape_squeeze.7.lengths, bf16[640,384]{1,0:T(8,128)(2,1)} %get-tuple-element.19.refs_0_.queries, bf16[640,384]{1,0:T(8,128)(2,1)} %copy-done.6, bf16[2,2048,768]{2,1,0:T(8,128)(2,1)} %refs_2_.3, ...), custom_call_target="tpu_custom_call" | custom-call | flops 5368709120 | bytes 12582912 | tf_op jit(solution)/shard_map/prefix/pallas_call | solution.py:267
  281.7 0.8 copy-done.7
  282.4 25.1 %prefix.3 = (bf16[640,512]{1,0:T(8,128)(2,1)}, bf16[640,512]{1,0:T(8,128)(2,1)}) custom-call(s32[8]{0:T(128)} %reshape_squeeze.6.starts, s32[8]{0:T(128)} %reshape_squeeze.7.lengths, bf16[640,384]{1,0:T(8,128)(2,1)} %get-tuple-element.26.refs_0_.queries, bf16[640,384]{1,0:T(8,128)(2,1)} %copy-done.7, bf16[2,2048,768]{2,1,0:T(8,128)(2,1)} %refs_2_.3, ...), custom_call_target="tpu_custom_call" | custom-call | flops 5368709120 | bytes 12582912 | tf_op jit(solution)/shard_map/prefix/pallas_call | solution.py:267
  307.6 0.9 reduce_sum.76.row_start
  308.5 7.7 %suffix.2 = (f32[640,384]{1,0:T(8,128)}, f32[640,128]{1,0:T(8,128)}) custom-call(s32[640,1]{1,0:T(8,128)} %reduce_sum.76.row_start, bf16[640,384]{1,0:T(8,128)(2,1)} %get-tuple-element.19.refs_0_.queries, bf16[640,384]{1,0:T(8,128)(2,1)} %get-tuple-element.22.keys, bf16[640,384]{1,0:T(8,128)(2,1)} %get-tuple-element.23.values), custom_call_target="tpu_custom_call" | custom-call | flops 1677721600 | bytes 2457600 | tf_op jit(solution)/shard_map/suffix/pallas_call | solution.py:334
  316.2 7.6 %suffix.3 = (f32[640,384]{1,0:T(8,128)}, f32[640,128]{1,0:T(8,128)}) custom-call(s32[640,1]{1,0:T(8,128)} %reduce_sum.76.row_start, bf16[640,384]{1,0:T(8,128)(2,1)} %get-tuple-element.26.refs_0_.queries, bf16[640,384]{1,0:T(8,128)(2,1)} %get-tuple-element.29.keys, bf16[640,384]{1,0:T(8,128)(2,1)} %get-tuple-element.30.values), custom_call_target="tpu_custom_call" | custom-call | flops 1677721600 | bytes 2457600 | tf_op jit(solution)/shard_map/suffix/pallas_call | solution.py:334
  323.8 0.8 copy-done.3
  324.6 7.9 %merge.2 = bf16[640,384]{1,0:T(8,128)(2,1)} custom-call(bf16[640,512]{1,0:T(8,128)(2,1)} %get-tuple-element.20.refs_0_, bf16[640,512]{1,0:T(8,128)(2,1)} %copy-done.3, f32[640,384]{1,0:T(8,128)} %get-tuple-element.24.refs_2_, f32[640,128]{1,0:T(8,128)} %get-tuple-element.25.refs_3_), custom_call_target="tpu_custom_call" | custom-call | flops 1966080 | bytes 2457600 | tf_op jit(solution)/shard_map/merge/pallas_call | solution.py:382
  332.6 0.5 collective-permute-start.13
  333.1 0.9 copy-done.4
  334.0 8.1 %merge.3 = bf16[640,384]{1,0:T(8,128)(2,1)} custom-call(bf16[640,512]{1,0:T(8,128)(2,1)} %get-tuple-element.27.refs_0_, bf16[640,512]{1,0:T(8,128)(2,1)} %copy-done.4, f32[640,384]{1,0:T(8,128)} %get-tuple-element.31.refs_2_, f32[640,128]{1,0:T(8,128)} %get-tuple-element.32.refs_3_), custom_call_target="tpu_custom_call" | custom-call | flops 1966080 | bytes 2457600 | tf_op jit(solution)/shard_map/merge/pallas_call | solution.py:382
  342.1 1.5 collective-permute-start.14
  343.6 5.8 %maximum_select_fusion = bf16[768,3072]{1,0:T(8,128)(2,1)S(1)} fusion(bf16[768,1536]{1,0:T(8,128)(2,1)} %collective-permute-done.16, bf16[768,1536]{1,0:T(8,128)(2,1)} %collective-permute-done.15, pred[]{:T(512)S(6)} %eq.42), kind=kLoop, calls=%fused_computation.22 | loop fusion | flops 21233664 | bytes 9437185 | tf_op jit(solution)/shard_map/jit(_where)/select_n | solution.py:495
  349.4 6.9 %collective-permute-done.14 = bf16[640,384]{1,0:T(8,128)(2,1)} collective-permute-done((bf16[640,384]{1,0:T(8,128)(2,1)}, bf16[640,384]{1,0:T(8,128)(2,1)}, u32[]{:S(2)}, u32[]{:S(2)}) %collective-permute-start.14) | collective-permute-done | bytes 491552 | tf_op jit(solution)/shard_map/ppermute | solution.py:431
  356.3 9.0 %fusion.6 = f32[640,3072]{1,0:T(8,128)S(1)} fusion(bf16[768,3072]{1,0:T(8,128)(2,1)S(1)} %maximum_select_fusion, bf16[768,768]{1,0:T(8,128)(2,1)} %get-tuple-element.38, bf16[768,768]{1,0:T(8,128)(2,1)} %get-tuple-element.39, bf16[768,768]{1,0:T(8,128)(2,1)} %get-tuple-element.40, bf16[768,768]{1,0:T(8,128)(2,1)} %get-tuple-element.35, ...), kind=kOutput, calls=%fused_computation.8 | convolution fusion | flops 6094848000 | bytes 19267584 | tf_op jit(solution)/shard_map/dot_general | solution.py:518
  365.4 3.1 copy-done.1
  368.4 0.3 dynamic-slice_convert_fusion.1
  368.7 1.3 collective-permute-start.17
  370.0 0.7 collective-permute-start.20
  370.7 22.5 %collective-permute-done.17 = bf16[640,768]{1,0:T(8,128)(2,1)} collective-permute-done((bf16[640,768]{1,0:T(8,128)(2,1)S(1)}, bf16[640,768]{1,0:T(8,128)(2,1)}, u32[]{:S(2)}, u32[]{:S(2)}) %collective-permute-start.17) | collective-permute-done | bytes 983072 | tf_op jit(solution)/shard_map/ppermute | solution.py:534
  393.3 2.1 add_convert_fusion.4
  395.3 1.9 collective-permute-start.18
  397.3 21.7 %collective-permute-done.18 = bf16[640,768]{1,0:T(8,128)(2,1)} collective-permute-done((bf16[640,768]{1,0:T(8,128)(2,1)S(1)}, bf16[640,768]{1,0:T(8,128)(2,1)}, u32[]{:S(2)}, u32[]{:S(2)}) %collective-permute-start.18) | collective-permute-done | bytes 983072 | tf_op jit(solution)/shard_map/ppermute | solution.py:534
  419.0 3.8 add_convert_fusion.3
  422.8 1.4 collective-permute-start.21
  424.2 4.6 collective-permute-start.19
  428.8 17.1 %collective-permute-done.21 = bf16[640,768]{1,0:T(8,128)(2,1)} collective-permute-done((bf16[640,768]{1,0:T(8,128)(2,1)}, bf16[640,768]{1,0:T(8,128)(2,1)}, u32[]{:S(2)}, u32[]{:S(2)}) %collective-permute-start.21) | collective-permute-done | bytes 983072 | tf_op jit(solution)/shard_map/ppermute | solution.py:535
  445.8 3.0 add_convert_fusion.1
  448.8 1.9 collective-permute-start.22
  450.8 20.0 %collective-permute-done.22 = bf16[640,768]{1,0:T(8,128)(2,1)} collective-permute-done((bf16[640,768]{1,0:T(8,128)(2,1)}, bf16[640,768]{1,0:T(8,128)(2,1)}, u32[]{:S(2)}, u32[]{:S(2)}) %collective-permute-start.22) | collective-permute-done | bytes 983072 | tf_op jit(solution)/shard_map/ppermute | solution.py:535
  470.8 3.3 add_convert_fusion
  (72 shorter events, 1.3 us)
Async XLA Ops:
  6.5 169.6 %all-gather.2.cloned.1.call-start = ((), (), s32[]{:S(2)}) async-start(), calls=%async_computation | async-start | bytes 8847360 | tf_op jit(solution)/shard_map/all_gather | solution.py:447
  13.9 160.6 %collective-permute-start.2 = (bf16[1536,1152]{1,0:T(8,128)(2,1)}, bf16[1536,1152]{1,0:T(8,128)(2,1)}, u32[]{:S(2)}, u32[]{:S(2)}) collective-permute-start(bf16[1536,1152]{1,0:T(8,128)(2,1)} %get-tuple-element.47.refs_0_), channel_id=1, source_target_pairs={{0,16},{8,24},{16,0},{24,8},{1,17},{9,25},{17,1},{25,9},{2,18},{10... | collective-permute-start | bytes 10616840 | tf_op jit(solution)/shard_map/ppermute | solution.py:424
  20.6 4.1 copy-start.14
  20.6 4.2 copy-start.12
  20.6 4.4 copy-start.13
  22.3 146.0 %collective-permute-start.15 = (bf16[768,1536]{1,0:T(8,128)(2,1)S(1)}, bf16[768,1536]{1,0:T(8,128)(2,1)}, u32[]{:S(2)}, u32[]{:S(2)}) collective-permute-start(bf16[768,1536]{1,0:T(8,128)(2,1)S(1)} %fusion.18), channel_id=1, source_target_pairs={{0,1},{1,0},{2,3},{3,2},{4,5},{5,4},{6,7},{7,6},{8,9},{9,8},{10,11... | collective-permute-start | bytes 7077896 | tf_op jit(solution)/shard_map/ppermute | solution.py:431
  22.9 157.8 %collective-permute-start.1 = (bf16[1536,1152]{1,0:T(8,128)(2,1)}, bf16[1536,1152]{1,0:T(8,128)(2,1)}, u32[]{:S(2)}, u32[]{:S(2)}) collective-permute-start(bf16[1536,1152]{1,0:T(8,128)(2,1)} %get-tuple-element.47.refs_0_), channel_id=1, source_target_pairs={{0,8},{8,0},{16,24},{24,16},{1,9},{9,1},{17,25},{25,17},{2,10},{10... | collective-permute-start | bytes 10616840 | tf_op jit(solution)/shard_map/ppermute | solution.py:421
  22.9 158.3 %collective-permute-start.9 = (bf16[1536,1152]{1,0:T(8,128)(2,1)}, bf16[1536,1152]{1,0:T(8,128)(2,1)}, u32[]{:S(2)}, u32[]{:S(2)}) collective-permute-start(bf16[1536,1152]{1,0:T(8,128)(2,1)} %get-tuple-element.48.refs_0_), channel_id=1, source_target_pairs={{0,16},{8,24},{16,0},{24,8},{1,17},{9,25},{17,1},{25,9},{2,18},{10... | collective-permute-start | bytes 10616840 | tf_op jit(solution)/shard_map/ppermute | solution.py:424
  25.1 143.2 %collective-permute-start = (s32[2,8]{1,0:T(2,128)S(1)}, s32[2,8]{1,0:T(2,128)S(1)}, u32[]{:S(2)}, u32[]{:S(2)}) collective-permute-start(s32[2,8]{1,0:T(2,128)S(1)} %pad_add_fusion.1), channel_id=1, source_target_pairs={{0,16},{8,24},{16,0},{24,8},{1,17},{9,25},{17,1},{25,9},{2,18},{10... | collective-permute-start | bytes 200 | tf_op jit(solution)/shard_map/ppermute | solution.py:424
  168.3 77.6 %collective-permute-start.5 = (bf16[2,2048,768]{2,1,0:T(8,128)(2,1)}, bf16[2,2048,768]{2,1,0:T(8,128)(2,1)}, u32[]{:S(2)}, u32[]{:S(2)}) collective-permute-start(bf16[2,2048,768]{2,1,0:T(8,128)(2,1)} %refs_2_.3), channel_id=1, source_target_pairs={{0,8},{8,0},{16,24},{24,16},{1,9},{9,1},{17,25},{25,17},{2,10},{10... | collective-permute-start | bytes 18874376 | tf_op jit(solution)/shard_map/ppermute | solution.py:421
  168.3 77.6 %collective-permute-start.6 = (bf16[2,2048,768]{2,1,0:T(8,128)(2,1)}, bf16[2,2048,768]{2,1,0:T(8,128)(2,1)}, u32[]{:S(2)}, u32[]{:S(2)}) collective-permute-start(bf16[2,2048,768]{2,1,0:T(8,128)(2,1)} %refs_4_.3), channel_id=1, source_target_pairs={{0,8},{8,0},{16,24},{24,16},{1,9},{9,1},{17,25},{25,17},{2,10},{10... | collective-permute-start | bytes 18874376 | tf_op jit(solution)/shard_map/ppermute | solution.py:421
  169.0 4.1 copy-start.10
  174.5 18.3 %collective-permute-start.3 = (bf16[1536,1152]{1,0:T(8,128)(2,1)}, bf16[1536,1152]{1,0:T(8,128)(2,1)}, u32[]{:S(2)}, u32[]{:S(2)}) collective-permute-start(bf16[1536,1152]{1,0:T(8,128)(2,1)} %collective-permute-done.2.refs_2_), channel_id=1, source_target_pairs={{0,8},{8,0},{16,24},{24,16},{1,9},{9,1},{17,25},{25,17},{2,10},{10... | collective-permute-start | bytes 10616840 | tf_op jit(solution)/shard_map/ppermute | solution.py:421
  176.1 5.5 %copy-start = (bf16[640,6144]{1,0:T(8,128)(2,1)S(1)}, bf16[640,6144]{1,0:T(8,128)(2,1)}, u32[]{:S(2)}) copy-start(bf16[640,6144]{1,0:T(8,128)(2,1)} %all-gather.2.cloned.1.call-done) | copy-start | bytes 23592964
  180.6 37.9 %collective-permute-start.8 = (bf16[1536,1152]{1,0:T(8,128)(2,1)}, bf16[1536,1152]{1,0:T(8,128)(2,1)}, u32[]{:S(2)}, u32[]{:S(2)}) collective-permute-start(bf16[1536,1152]{1,0:T(8,128)(2,1)} %get-tuple-element.48.refs_0_), channel_id=1, source_target_pairs={{0,8},{8,0},{16,24},{24,16},{1,9},{9,1},{17,25},{25,17},{2,10},{10... | collective-permute-start | bytes 10616840 | tf_op jit(solution)/shard_map/ppermute | solution.py:421
  181.2 37.9 %collective-permute-start.10 = (bf16[1536,1152]{1,0:T(8,128)(2,1)}, bf16[1536,1152]{1,0:T(8,128)(2,1)}, u32[]{:S(2)}, u32[]{:S(2)}) collective-permute-start(bf16[1536,1152]{1,0:T(8,128)(2,1)} %collective-permute-done.9.refs_2_), channel_id=1, source_target_pairs={{0,8},{8,0},{16,24},{24,16},{1,9},{9,1},{17,25},{25,17},{2,10},{10... | collective-permute-start | bytes 10616840 | tf_op jit(solution)/shard_map/ppermute | solution.py:421
  181.6 2.2 copy-start.8
  181.6 2.2 copy-start.9
  192.9 150.7 %collective-permute-start.16 = (bf16[768,1536]{1,0:T(8,128)(2,1)}, bf16[768,1536]{1,0:T(8,128)(2,1)}, u32[]{:S(2)}, u32[]{:S(2)}) collective-permute-start(bf16[768,1536]{1,0:T(8,128)(2,1)} %collective-permute-done.15), channel_id=1, source_target_pairs={{0,8},{8,0},{16,24},{24,16},{1,9},{9,1},{17,25},{25,17},{2,10},{10... | collective-permute-start | bytes 7077896 | tf_op jit(solution)/shard_map/ppermute | solution.py:421
  218.5 27.4 %collective-permute-start.4 = (bf16[640,384]{1,0:T(8,128)(2,1)}, bf16[640,384]{1,0:T(8,128)(2,1)S(1)}, u32[]{:S(2)}, u32[]{:S(2)}) collective-permute-start(bf16[640,384]{1,0:T(8,128)(2,1)} %get-tuple-element.19.refs_0_.queries), channel_id=1, source_target_pairs={{0,16},{8,24},{16,0},{24,8},{1,17},{9,25},{17,1},{25,9},{2,18},{10... | collective-permute-start | bytes 1474568 | tf_op jit(solution)/shard_map/ppermute | solution.py:424
  244.4 37.3 %collective-permute-start.11 = (bf16[640,384]{1,0:T(8,128)(2,1)}, bf16[640,384]{1,0:T(8,128)(2,1)S(1)}, u32[]{:S(2)}, u32[]{:S(2)}) collective-permute-start(bf16[640,384]{1,0:T(8,128)(2,1)} %get-tuple-element.26.refs_0_.queries), channel_id=1, source_target_pairs={{0,16},{8,24},{16,0},{24,8},{1,17},{9,25},{17,1},{25,9},{2,18},{10... | collective-permute-start | bytes 1474568 | tf_op jit(solution)/shard_map/ppermute | solution.py:424
  245.9 0.8 copy-start.6
  281.6 42.2 %collective-permute-start.7 = (bf16[640,512]{1,0:T(8,128)(2,1)}, bf16[640,512]{1,0:T(8,128)(2,1)S(1)}, u32[]{:S(2)}, u32[]{:S(2)}) collective-permute-start(bf16[640,512]{1,0:T(8,128)(2,1)} %get-tuple-element.21), channel_id=1, source_target_pairs={{0,16},{8,24},{16,0},{24,8},{1,17},{9,25},{17,1},{25,9},{2,18},{10... | collective-permute-start | bytes 1966088 | tf_op jit(solution)/shard_map/ppermute | solution.py:424
  281.6 0.8 copy-start.7
  307.5 25.6 %collective-permute-start.12 = (bf16[640,512]{1,0:T(8,128)(2,1)}, bf16[640,512]{1,0:T(8,128)(2,1)S(1)}, u32[]{:S(2)}, u32[]{:S(2)}) collective-permute-start(bf16[640,512]{1,0:T(8,128)(2,1)} %get-tuple-element.28), channel_id=1, source_target_pairs={{0,16},{8,24},{16,0},{24,8},{1,17},{9,25},{17,1},{25,9},{2,18},{10... | collective-permute-start | bytes 1966088 | tf_op jit(solution)/shard_map/ppermute | solution.py:424
  323.8 0.8 copy-start.3
  332.6 16.8 %collective-permute-start.13 = (bf16[640,384]{1,0:T(8,128)(2,1)}, bf16[640,384]{1,0:T(8,128)(2,1)}, u32[]{:S(2)}, u32[]{:S(2)}) collective-permute-start(bf16[640,384]{1,0:T(8,128)(2,1)} %merge.2), channel_id=1, source_target_pairs={{0,1},{1,0},{2,3},{3,2},{4,5},{5,4},{6,7},{7,6},{8,9},{9,8},{10,11... | collective-permute-start | bytes 1474568 | tf_op jit(solution)/shard_map/ppermute | solution.py:431
  333.1 0.9 copy-start.4
  342.1 14.2 %collective-permute-start.14 = (bf16[640,384]{1,0:T(8,128)(2,1)}, bf16[640,384]{1,0:T(8,128)(2,1)}, u32[]{:S(2)}, u32[]{:S(2)}) collective-permute-start(bf16[640,384]{1,0:T(8,128)(2,1)} %merge.3), channel_id=1, source_target_pairs={{0,1},{1,0},{2,3},{3,2},{4,5},{5,4},{6,7},{7,6},{8,9},{9,8},{10,11... | collective-permute-start | bytes 1474568 | tf_op jit(solution)/shard_map/ppermute | solution.py:431
  343.6 12.7 %copy-start.5 = (bf16[640,384]{1,0:T(8,128)(2,1)S(1)}, bf16[640,384]{1,0:T(8,128)(2,1)}, u32[]{:S(2)}) copy-start(bf16[640,384]{1,0:T(8,128)(2,1)} %merge.2) | copy-start | bytes 1474564
  365.4 3.1 copy-start.1
  368.7 24.6 %collective-permute-start.17 = (bf16[640,768]{1,0:T(8,128)(2,1)S(1)}, bf16[640,768]{1,0:T(8,128)(2,1)}, u32[]{:S(2)}, u32[]{:S(2)}) collective-permute-start(bf16[640,768]{1,0:T(8,128)(2,1)S(1)} %get-tuple-element.45), channel_id=1, source_target_pairs={{0,2},{1,3},{8,10},{9,11},{16,18},{17,19},{24,26},{25,27}} | collective-permute-start | bytes 2949128 | tf_op jit(solution)/shard_map/ppermute | solution.py:534
  370.0 27.3 %collective-permute-start.20 = (bf16[640,768]{1,0:T(8,128)(2,1)S(1)}, bf16[640,768]{1,0:T(8,128)(2,1)S(1)}, u32[]{:S(2)}, u32[]{:S(2)}) collective-permute-start(bf16[640,768]{1,0:T(8,128)(2,1)S(1)} %get-tuple-element.46), channel_id=1, source_target_pairs={{6,4},{7,5},{14,12},{15,13},{22,20},{23,21},{30,28},{31,29}} | collective-permute-start | bytes 2949128 | tf_op jit(solution)/shard_map/ppermute | solution.py:535
  395.3 23.6 %collective-permute-start.18 = (bf16[640,768]{1,0:T(8,128)(2,1)S(1)}, bf16[640,768]{1,0:T(8,128)(2,1)}, u32[]{:S(2)}, u32[]{:S(2)}) collective-permute-start(bf16[640,768]{1,0:T(8,128)(2,1)S(1)} %add_convert_fusion.4), channel_id=1, source_target_pairs={{0,2},{1,3},{2,4},{3,5},{8,10},{9,11},{10,12},{11,13},{16,18},{17,... | collective-permute-start | bytes 2949128 | tf_op jit(solution)/shard_map/ppermute | solution.py:534
  422.8 28.0 %copy-start.11 = (bf16[768]{0:T(1024)(128)(2,1)S(1)}, bf16[768]{0:T(1024)(128)(2,1)}, u32[]{:S(2)}) copy-start(bf16[768]{0:T(1024)(128)(2,1)} %param.18) | copy-start | bytes 4612
  422.8 48.1 %copy-start.2 = (bf16[640,768]{1,0:T(8,128)(2,1)S(1)}, bf16[640,768]{1,0:T(8,128)(2,1)}, u32[]{:S(2)}) copy-start(bf16[640,768]{1,0:T(8,128)(2,1)} %param.12) | copy-start | bytes 2949124
  422.8 23.1 %collective-permute-start.21 = (bf16[640,768]{1,0:T(8,128)(2,1)}, bf16[640,768]{1,0:T(8,128)(2,1)}, u32[]{:S(2)}, u32[]{:S(2)}) collective-permute-start(bf16[640,768]{1,0:T(8,128)(2,1)} %get-tuple-element.44), channel_id=1, source_target_pairs={{4,2},{5,3},{6,4},{7,5},{12,10},{13,11},{14,12},{15,13},{20,18},{2... | collective-permute-start | bytes 2949128 | tf_op jit(solution)/shard_map/ppermute | solution.py:535
  424.2 26.6 %collective-permute-start.19 = (bf16[640,768]{1,0:T(8,128)(2,1)S(1)}, bf16[640,768]{1,0:T(8,128)(2,1)S(1)}, u32[]{:S(2)}, u32[]{:S(2)}) collective-permute-start(bf16[640,768]{1,0:T(8,128)(2,1)S(1)} %get-tuple-element.43), channel_id=1, source_target_pairs={{0,2},{1,3},{2,4},{3,5},{4,6},{5,7},{8,10},{9,11},{10,12},{11,13},... | collective-permute-start | bytes 2949128 | tf_op jit(solution)/shard_map/ppermute | solution.py:534
  448.8 22.0 %collective-permute-start.22 = (bf16[640,768]{1,0:T(8,128)(2,1)}, bf16[640,768]{1,0:T(8,128)(2,1)}, u32[]{:S(2)}, u32[]{:S(2)}) collective-permute-start(bf16[640,768]{1,0:T(8,128)(2,1)} %add_convert_fusion.1), channel_id=1, source_target_pairs={{2,0},{3,1},{4,2},{5,3},{6,4},{7,5},{10,8},{11,9},{12,10},{13,11},... | collective-permute-start | bytes 2949128 | tf_op jit(solution)/shard_map/ppermute | solution.py:535
Sparse Core Ops, SparseCore 0:
  9.5 138.4 all-gather.1

commit v2 on v1

--- a/solution.py
+++ b/solution.py
@@ -37,11 +37,33 @@
     return pltpu.CompilerParams(vmem_limit_bytes=VMEM_LIMIT)
 
 
-def layer_norm(values_in, gain, shift):
-    widened = values_in.astype(F32)
+def norm_kernel(values, gain, shift, out):
+    widened = values[...].astype(F32)
     center = jnp.mean(widened, axis=-1, keepdims=True)
-    spread = jnp.mean(jnp.square(widened - center), axis=-1, keepdims=True)
-    return ((widened - center) * lax.rsqrt(spread + 1e-05) * gain + shift).astype(BF16)
+    moved = widened - center
+    spread = jnp.mean(jnp.square(moved), axis=-1, keepdims=True)
+    out[...] = (moved * lax.rsqrt(spread + 1e-05) * gain[...] + shift[...]).astype(BF16)
+
+
+def layer_norm(values, gain, shift):
+    rows, features = values.shape
+    tile = 64
+    return pl.pallas_call(
+        norm_kernel,
+        out_shape=jax.ShapeDtypeStruct((rows, features), BF16),
+        grid=(rows // tile,),
+        in_specs=[
+            pl.BlockSpec((tile, features), lambda i: (i, 0)),
+            pl.BlockSpec((1, features), lambda i: (0, 0)),
+            pl.BlockSpec((1, features), lambda i: (0, 0)),
+        ],
+        out_specs=pl.BlockSpec((tile, features), lambda i: (i, 0)),
+        compiler_params=params(),
+        cost_estimate=pl.CostEstimate(
+            flops=rows * features * 8, bytes_accessed=rows * features * 4, transcendentals=rows
+        ),
+        name="norm",
+    )(values, gain[None, :], shift[None, :])
 
 
 def shard_layout(lengths, ordering, row_count):
@@ -76,48 +98,67 @@
 
 def qkv_kernel(pieces, order, normed, *refs):
     weights = refs[:pieces]
-    bias, straight, upper, lower, q_out, k_out, v_out, total = refs[pieces:]
-    step = pl.program_id(0)
-    depth = weights[0].shape[0]
-    summed = None
+    bias, straight, upper, lower, q_out, k_out, v_out = refs[pieces : pieces + 7]
+    total, held_rows, held_weights, row_sems, weight_sems = refs[pieces + 7 :]
+    depth, columns = weights[0].shape
+
+    def row_copy(j):
+        lanes = pl.ds(pl.multiple_of(order[j] * depth, 128), depth)
+        return pltpu.make_async_copy(normed.at[:, lanes], held_rows.at[j], row_sems.at[j])
+
+    def weight_copy(j):
+        return pltpu.make_async_copy(weights[j], held_weights.at[j], weight_sems.at[j])
+
     for j in range(pieces):
-        columns = pl.ds(pl.multiple_of(order[j] * depth, 128), depth)
-        part = jnp.dot(normed[:, columns], weights[j][...], preferred_element_type=F32)
-        summed = part if summed is None else summed + part
-    total[step] = summed + bias[...]
-
-    @pl.when(step == 2)
-    def _():
-        tile = 64
-
-        def body(i, carry):
-            rows = pl.ds(pl.multiple_of(i * tile, tile), tile)
-            wide = jnp.concatenate([total[n, rows, :] for n in range(3)], axis=1)
-
-            def part(c):
-                result = None
-                for k in range(GROUP_HEADS):
-                    first = 192 * k + HS * c
-                    cut = wide[:, first : first + GW]
-                    if result is None:
-                        result = cut
+        row_copy(j).start()
+        weight_copy(j).start()
+    for j in range(pieces):
+        row_copy(j).wait()
+        weight_copy(j).wait()
+        for first in range(0, columns, 256):
+            lanes = slice(first, min(first + 256, columns))
+            part = jnp.dot(
+                held_rows[j], held_weights[j, :, lanes], preferred_element_type=F32
+            )
+            if j == 0:
+                total[:, lanes] = part + bias[:, lanes]
+            else:
+                total[:, lanes] += part
+
+    tile = 64
+
+    def body(i, carry):
+        rows = pl.ds(pl.multiple_of(i * tile, tile), tile)
+        wide = total[rows, :]
+
+        def part(c):
+            merged = [None] * (GW // 128)
+            for k, (first, width) in enumerate(windows()):
+                source = 192 * k + HS * c + first
+                cut = wide[:, source : source + width]
+                mask = head_mask(k, first, cut.shape)
+                for w in range(width // 128):
+                    at = first // 128 + w
+                    lanes = slice(w * 128, w * 128 + 128)
+                    if merged[at] is None:
+                        merged[at] = cut[:, lanes]
                     else:
-                        result = jnp.where(head_mask(k, 0, cut.shape), cut, result)
-                return result
-
-            def turn(x):
-                return (
-                    x * straight[rows, :]
-                    + pltpu.roll(x, GW - HS // 8, 1) * upper[rows, :]
-                    + pltpu.roll(x, HS // 8, 1) * lower[rows, :]
-                )
-
-            q_out[rows, :] = turn(part(0)).astype(BF16)
-            k_out[rows, :] = turn(part(1)).astype(BF16)
-            v_out[rows, :] = part(2).astype(BF16)
-            return carry
-
-        lax.fori_loop(0, total.shape[1] // tile, body, 0)
+                        merged[at] = jnp.where(mask[:, lanes], cut[:, lanes], merged[at])
+            return jnp.concatenate(merged, axis=1)
+
+        def turn(x):
+            return (
+                x * straight[rows, :]
+                + pltpu.roll(x, GW - HS // 8, 1) * upper[rows, :]
+                + pltpu.roll(x, HS // 8, 1) * lower[rows, :]
+            )
+
+        q_out[rows, :] = turn(part(0)).astype(BF16)
+        k_out[rows, :] = turn(part(1)).astype(BF16)
+        v_out[rows, :] = part(2).astype(BF16)
+        return carry
+
+    lax.fori_loop(0, total.shape[0] // tile, body, 0)
 
 
 def project(normed, weights, order, bias, tables):
@@ -125,21 +166,22 @@
     pieces = len(weights)
     depth, columns = weights[0].shape
     out = jax.ShapeDtypeStruct((rows, GW), BF16)
-    whole = lambda n, order: (0, 0)
-    tile = lambda n, order: (0, n)
+    vmem = pl.BlockSpec(memory_space=pltpu.VMEM)
+    anywhere = pl.BlockSpec(memory_space=pl.ANY)
     return pl.pallas_call(
         functools.partial(qkv_kernel, pieces),
         out_shape=(out, out, out),
-        grid_spec=pltpu.PrefetchScalarGridSpec(
-            num_scalar_prefetch=1,
-            grid=(columns // GW,),
-            in_specs=[pl.BlockSpec((rows, features), whole)]
-            + [pl.BlockSpec((depth, GW), tile)] * pieces
-            + [pl.BlockSpec((1, GW), tile)]
-            + [pl.BlockSpec((rows, GW), whole)] * 3,
-            out_specs=[pl.BlockSpec((rows, GW), whole)] * 3,
-            scratch_shapes=[pltpu.VMEM((columns // GW, rows, GW), F32)],
-        ),
+        in_specs=[pl.BlockSpec(memory_space=pltpu.SMEM)]
+        + [anywhere] * (pieces + 1)
+        + [vmem] * 4,
+        out_specs=[vmem] * 3,
+        scratch_shapes=[
+            pltpu.VMEM((rows, columns), F32),
+            pltpu.VMEM((pieces, rows, depth), BF16),
+            pltpu.VMEM((pieces, depth, columns), BF16),
+            pltpu.SemaphoreType.DMA((pieces,)),
+            pltpu.SemaphoreType.DMA((pieces,)),
+        ],
         compiler_params=params(),
         cost_estimate=pl.CostEstimate(
             flops=2 * rows * features * columns,
@@ -217,7 +259,7 @@
                 middle = (level - high).astype(BF16).astype(F32)
                 low = level - high - middle
                 for n, term in enumerate((high, middle, low)):
-                    extra = jnp.where(place == 3 * k + n, term, extra)
+                    extra = jnp.where(place == 32 * n + k, term, extra)
             packed = jnp.concatenate(merged + [extra], axis=1).astype(BF16)
             for b in range(blocks):
                 spread = lax.broadcasted_iota(jnp.int32, (rows, height), 0)
@@ -357,24 +399,17 @@
         prefix = parts[0][at, :].astype(F32)
         for b in range(1, blocks):
             prefix = prefix + parts[b][at, :].astype(F32)
-        share_pre = jnp.zeros((tile, GW), F32)
-        share_suf = jnp.zeros((tile, GW), F32)
+        terms = prefix[:, GW:]
+        pre = terms + pltpu.roll(terms, PACK - 32, 1) + pltpu.roll(terms, PACK - 64, 1)
+        suf = levels[at, :]
+        top = jnp.maximum(pre, suf)
+        pre = jnp.exp(pre - top)
+        suf = jnp.exp(suf - top)
+        shares = pre / (pre + suf)
+        spread = jnp.zeros((tile, GW), F32)
         for k in range(GROUP_HEADS):
-            lane = GW + 3 * k
-            pre = (
-                prefix[:, lane : lane + 1]
-                + prefix[:, lane + 1 : lane + 2]
-                + prefix[:, lane + 2 : lane + 3]
-            )
-            suf = levels[at, k : k + 1]
-            top = jnp.maximum(pre, suf)
-            pre = jnp.exp(pre - top)
-            suf = jnp.exp(suf - top)
-            whole = 1.0 / (pre + suf)
-            mask = head_mask(k, 0, (tile, GW))
-            share_pre = jnp.where(mask, pre * whole, share_pre)
-            share_suf = jnp.where(mask, suf * whole, share_suf)
-        out[at, :] = (share_pre * prefix[:, :GW] + share_suf * suffix[at, :]).astype(BF16)
+            spread = jnp.where(head_mask(k, 0, (tile, GW)), shares[:, k : k + 1], spread)
+        out[at, :] = (spread * prefix[:, :GW] + (1.0 - spread) * suffix[at, :]).astype(BF16)
 
 
 def merge(parts, suffix, levels):
@@ -430,6 +465,10 @@
     def to_side(x):
         return lax.ppermute(x, "head", [(h, h ^ 1) for h in range(head_size)])
 
+    layout = jnp.stack([suffix_len[0], request_order[0]])
+    layouts = [layout] + [to_chip(layout, shift) for shift in range(1, chips)]
+    full_rows = lax.all_gather(hidden_states, "head", axis=1, tiled=True)
+
     columns = 3 * GW
     order = [tok, tok ^ 1]
     for shift in range(1, chips):
@@ -437,40 +476,44 @@
         order += [source, source ^ 1]
     order = jnp.stack(order).astype(jnp.int32)
     gathered = []
+    earlier = layouts
+    source = qkv_weight
     for g in range(groups_local):
-        mine = qkv_weight[:, g * columns : (g + 1) * columns]
+        mine = source[:, g * columns : (g + 1) * columns]
+        mine, earlier = lax.optimization_barrier((mine, earlier))
+        if g == 0:
+            layouts = earlier
+            source, _ = lax.optimization_barrier((qkv_weight, layouts))
+        arrived = [to_chip(mine, shift) for shift in range(1, chips)]
         pieces = [mine, to_core(mine)]
-        for shift in range(1, chips):
-            arrived = to_chip(mine, shift)
-            pieces += [arrived, to_core(arrived)]
+        for one in arrived:
+            pieces += [one, to_core(one)]
         gathered.append(pieces)
-    full_rows = lax.all_gather(hidden_states, "head", axis=1, tiled=True)
+        earlier = arrived
     cache = [prefix_keys, to_core(prefix_keys), prefix_values, to_core(prefix_values)]
 
     lengths = suffix_len[0]
     starts, row_start, within = shard_layout(lengths, request_order[0], rows)
     labels = jnp.arange(group_count, dtype=jnp.int32)
     slot_match = (group_slot[:, None] == labels[None, :]).astype(jnp.int32)
-    spans = jnp.stack(
-        [
-            jnp.sum(starts[:, None] * slot_match, axis=0),
-            jnp.sum(lengths[:, None] * slot_match, axis=0),
-        ]
-    )
-    all_spans = [spans] + [to_chip(spans, shift) for shift in range(1, chips)]
-    served = jnp.stack(
-        [
-            jnp.concatenate(
-                [
-                    lax.dynamic_slice(one, (0, tok * held), (2, held)),
-                    lax.dynamic_slice(one, (0, (tok ^ 1) * held), (2, held)),
-                ],
-                axis=1,
-            )
-            for one in all_spans
-        ],
-        axis=2,
-    )
+
+    def served_spans(one):
+        firsts = shard_layout(one[0], one[1], rows)[0]
+        spans = jnp.stack(
+            [
+                jnp.sum(firsts[:, None] * slot_match, axis=0),
+                jnp.sum(one[0][:, None] * slot_match, axis=0),
+            ]
+        )
+        return jnp.concatenate(
+            [
+                lax.dynamic_slice(spans, (0, tok * held), (2, held)),
+                lax.dynamic_slice(spans, (0, (tok ^ 1) * held), (2, held)),
+            ],
+            axis=1,
+        )
+
+    served = jnp.stack([served_spans(one) for one in layouts], axis=2)
     span_start = served[0].reshape(-1)
     span_length = served[1].reshape(-1)
     tables = rotary_tables(prefix_length + within)
@@ -490,6 +533,7 @@
         (0, core * half * share),
         (dense_weight.shape[0], half * share),
     )
+    outgoing, full_rows = lax.optimization_barrier((outgoing, full_rows))
     landed = to_side(outgoing)
     crossed = to_core(landed)
     received = jnp.where(
@@ -511,30 +555,46 @@
         answers = prefix_attention(g, asked, cache, span_start, span_length)
         parts = [answers[0]] + [to_chip(answers[s], chips - s) for s in range(1, chips)]
         suffix, levels = suffix_attention(row_start[:, None], queries, keys, values)
+        if g == groups_local - 1:
+            levels, dense_both = lax.optimization_barrier((levels, dense_both))
         attention = merge(parts, suffix, levels)
         attention_own.append(attention)
         attention_side.append(to_side(attention))
     attention = jnp.concatenate(attention_own + attention_side, axis=1)
     partial = jnp.dot(attention, dense_both, preferred_element_type=F32)
 
-    def chunk(place):
-        place = jnp.clip(place, 0, lines - 1)
-        return lax.dynamic_slice(partial, (0, place * share), (rows, share))
-
-    upward = downward = None
     last = lines - 1
+    cuts = 2
+    height = rows // cuts
+
+    def chunk(place, cut):
+        place = jnp.clip(place, 0, last)
+        return lax.dynamic_slice(partial, (cut * height, place * share), (height, share))
+
+    passing = [None] * cuts
     for step in range(last):
-        up = chunk(last + line - step)
-        down = chunk(line - last + step)
-        if upward is not None:
-            up = up + upward.astype(F32)
-            down = down + downward.astype(F32)
         up_pairs = [(h, h + 2) for h in range(head_size) if h // 2 <= step and h // 2 < last]
         down_pairs = [(h, h - 2) for h in range(head_size) if last - h // 2 <= step and h // 2 > 0]
-        upward = lax.ppermute(up.astype(BF16), "head", up_pairs)
-        downward = lax.ppermute(down.astype(BF16), "head", down_pairs)
-    summed = chunk(line) + upward.astype(F32) + downward.astype(F32)
-    return (hidden_states.astype(F32) + dense_bias.astype(F32) + summed).astype(BF16)
+        for cut in range(cuts):
+            up = chunk(last + line - step, cut)
+            down = chunk(line - last + step, cut)
+            if passing[cut] is not None:
+                if cut > 0:
+                    passing[cut], sent = lax.optimization_barrier((passing[cut], sent))
+                up = up + passing[cut][0].astype(F32)
+                down = down + passing[cut][1].astype(F32)
+            up, down = lax.optimization_barrier((up.astype(BF16), down.astype(BF16)))
+            sent = up
+            passing[cut] = lax.optimization_barrier(
+                (lax.ppermute(up, "head", up_pairs), lax.ppermute(down, "head", down_pairs))
+            )
+    base = hidden_states.astype(F32) + dense_bias.astype(F32)
+    done = [
+        base[cut * height : (cut + 1) * height]
+        + (chunk(line, cut) + passing[cut][0].astype(F32) + passing[cut][1].astype(F32))
+        for cut in range(cuts)
+    ]
+    return jnp.concatenate(done, axis=0).astype(BF16)
 
 
 def solution(mesh):

time: 490 us -> 521 us (1.063)
  other arithmetic: 35.5 us -> 61.1 us
  waiting for transfers between devices: 233 us -> 214 us
  starting transfers between devices: 20.5 us -> 38 us
  local copies, waits for them, and re-layouts: 27.1 us -> 37.6 us
    ppermute x6 -> x12, waiting for transfers between devices: 81.3 us -> 43 us  [the longest x6 32.4 us: on_device(): lax.ppermute(up, 'head', up_pairs)]
    concatenate x0 -> x2, other arithmetic: none -> 38.2 us  [the longest x1 37.2 us: on_device(): jnp.concatenate([jnp.concatenate(side_columns(side), axis=1), received],...]
    ppermute x3, waiting for transfers between devices: 6.95 us -> 30.3 us  [to_side(): return lax.ppermute(x, 'head', [(h, h ^ 1) for h in range(head_size)])]
    ppermute x6 -> x12, starting transfers between devices: 11.8 us -> 29.1 us  [the longest x6 17.8 us: on_device(): lax.ppermute(up, 'head', up_pairs)]
    convert_element_type x6 -> x4, other arithmetic: 19.9 us -> 7.06 us  [the longest x3 7.06 us: on_device(): up, down = lax.optimization_barrier((up.astype(BF16), down.astype(BF16)))]
    pallas_call x0 -> x1, Pallas kernels: none -> 12.8 us  [layer_norm(): pl.pallas_call(norm_kernel, out_shape=jax.ShapeDtypeStruct((rows, feature...]
    another operation x6, local copies, waits for them, and re-layouts: 4.12 us -> 13.4 us  [rotary_tables(): jnp.tile(table, (1, GROUP_HEADS))]
    pallas_call x2, Pallas kernels: 16.1 us -> 7.22 us  [merge(): pl.pallas_call(functools.partial(merge_kernel, len(parts)), out_shape=jax...]
  transfers between devices with their start and end apart: 24 -> 30, of which waited for: 7 -> 13; matrix products, arithmetic and copies ran while one was open for 10% -> 17% of each run, Pallas kernels for 30% -> 28%
where the time goes in v2:
time: 521 us; the launch traced here: 516 us
  waiting for transfers between devices  214 us (41%)
  Pallas kernels  142 us (27%)
  other arithmetic  61.1 us (12%)
  starting transfers between devices  38 us (7%)
  local copies, waits for them, and re-layouts  37.6 us (7%)
  between operations  14 us (3%)
  matrix products  9.19 us (2%)
    ppermute x7, waiting for transfers between devices, to_chip(): lax.ppermute(x, 'tok', [(t, (t // 2 + shift) % chips * 2 + t % 2) for t i...  140 us
    pallas_call x2, Pallas kernels, prefix_attention(): pl.pallas_call(functools.partial(prefix_kernel, blocks), out_shape=[jax.S...  60.2 us
    pallas_call x2, Pallas kernels, project(): pl.pallas_call(functools.partial(qkv_kernel, pieces), out_shape=(out, out...  46.6 us
    concatenate x1, other arithmetic, on_device(): jnp.concatenate([jnp.concatenate(side_columns(side), axis=1), received],...  37.2 us
    ppermute x6, waiting for transfers between devices, on_device(): lax.ppermute(up, 'head', up_pairs)  32.4 us
    ppermute x3, waiting for transfers between devices, to_side(): return lax.ppermute(x, 'head', [(h, h ^ 1) for h in range(head_size)])  30.3 us
    ppermute x6, starting transfers between devices, on_device(): lax.ppermute(up, 'head', up_pairs)  17.8 us
    pallas_call x2, Pallas kernels, suffix_attention(): pl.pallas_call(suffix_kernel, out_shape=(jax.ShapeDtypeStruct((rows, GW),...  15.3 us
  transfers between devices with their start and end apart: 30, of which 13 were waited for; matrix products, arithmetic and copies ran while one was open for 17% of the time, Pallas kernels for 28%

profile of v2, /device:TPU:14, one launch (start us, length us, event | category | flops | bytes accessed | tf_op | source)
XLA Modules:
  0.0 516.3 jit_solution(5059116909483160126)
XLA Ops:
  7.3 0.8 pad_add_fusion.1
  8.6 4.3 slice.39.refs_0_
  13.0 1.3 collective-permute-start.2
  14.2 2.1 slice.47.refs_0_
  16.3 74.9 %collective-permute-done.2.refs_2_ = bf16[1536,1152]{1,0:T(8,128)(2,1)} collective-permute-done((bf16[1536,1152]{1,0:T(8,128)(2,1)}, bf16[1536,1152]{1,0:T(8,128)(2,1)}, u32[]{:S(2)}, u32[]{:S(2)}) %collective-permute-start.2) | collective-permute-done | bytes 3538976 | tf_op jit(solution)/shard_map/ppermute | solution.py:459
  91.2 1.3 collective-permute-start.9
  94.7 5.4 %constant_dynamic-slice_fusion.3 = (bf16[768,768]{1,0:T(8,128)(2,1)S(1)}, bf16[768,768]{1,0:T(8,128)(2,1)S(1)}, bf16[768,768]{1,0:T(8,128)(2,1)S(1)}, bf16[768,7...) fusion(bf16[768,6144]{1,0:T(8,128)(2,1)} %param.17, ...), kind=kLoop, calls=%fused_computation.48 | loop fusion | bytes 18874400 | tf_op jit(solution)/shard_map/dynamic_slice | solution.py:524
  100.1 2.6 fusion.2
  103.3 65.2 %collective-permute-done.9.refs_2_ = bf16[1536,1152]{1,0:T(8,128)(2,1)} collective-permute-done((bf16[1536,1152]{1,0:T(8,128)(2,1)}, bf16[1536,1152]{1,0:T(8,128)(2,1)}, u32[]{:S(2)}, u32[]{:S(2)}) %collective-permute-start.9) | collective-permute-done | bytes 3538976 | tf_op jit(solution)/shard_map/ppermute | solution.py:459
  168.5 0.9 multiply_sine_fusion
  169.9 1.8 maximum_maximum_fusion.2
  171.8 0.9 reduce_sum.116.row_start
  172.6 2.0 tile.12
  174.6 2.5 copy.27.refs_5_
  177.1 2.0 tile.14
  179.0 2.5 copy.28.refs_6_
  181.5 2.0 tile.31
  183.5 2.5 copy.29.refs_7_
  188.9 0.8 select_reduce_fusion.4
  192.3 12.8 %norm.1.normed = bf16[640,6144]{1,0:T(8,128)(2,1)} custom-call(bf16[640,6144]{1,0:T(8,128)(2,1)} %all-gather.2.cloned.1.call-done.values, f32[1,6144]{1,0:T(1,128)} %bitcast.37, f32[1,6144]{1,0:T(1,128)} %bitcast.38), custom_call_target="tpu_custom_call" | custom-call | flops 31457280 | bytes 15728640 | tf_op jit(solution)/shard_map/norm/pallas_call | solution.py:51
  205.1 18.2 %collective-permute-done.13 = bf16[768,1536]{1,0:T(8,128)(2,1)} collective-permute-done((bf16[768,1536]{1,0:T(8,128)(2,1)}, bf16[768,1536]{1,0:T(8,128)(2,1)}, u32[]{:S(2)}, u32[]{:S(2)}) %collective-permute-start.13) | collective-permute-done | bytes 2359328 | tf_op jit(solution)/shard_map/ppermute | solution.py:466
  223.3 23.3 %project.2 = (bf16[640,384]{1,0:T(8,128)(2,1)}, bf16[640,384]{1,0:T(8,128)(2,1)}, bf16[640,384]{1,0:T(8,128)(2,1)}) custom-call(s32[4]{0:T(128)} %pad_add_fusion.4.order, bf16[640,6144]{1,0:T(8,128)(2,1)} %norm.1.normed, bf16[1536,1152]{1,0:T(8,128)(2,1)} %slice.39.refs_0_, bf16[1536,1152]{1,0:T(8,128)(2,1)} %collective-permute-done.1.refs_1_, ...), custom_call_target="tpu_custom_call" | custom-call | flops 9059696640 | bytes 26443776 | tf_op jit(solution)/shard_map/project/pallas_call | solution.py:171
  246.7 1.5 collective-permute-start.4
  248.2 23.3 %project.3 = (bf16[640,384]{1,0:T(8,128)(2,1)}, bf16[640,384]{1,0:T(8,128)(2,1)}, bf16[640,384]{1,0:T(8,128)(2,1)}) custom-call(s32[4]{0:T(128)} %pad_add_fusion.4.order, bf16[640,6144]{1,0:T(8,128)(2,1)} %norm.1.normed, bf16[1536,1152]{1,0:T(8,128)(2,1)} %slice.47.refs_0_, bf16[1536,1152]{1,0:T(8,128)(2,1)} %collective-permute-done.8.refs_1_, ...), custom_call_target="tpu_custom_call" | custom-call | flops 9059696640 | bytes 26443776 | tf_op jit(solution)/shard_map/project/pallas_call | solution.py:171
  272.2 7.7 %suffix.2 = (f32[640,384]{1,0:T(8,128)}, f32[640,128]{1,0:T(8,128)}) custom-call(s32[640,1]{1,0:T(8,128)} %reduce_sum.116.row_start, bf16[640,384]{1,0:T(8,128)(2,1)} %get-tuple-element.60.refs_0_.queries, bf16[640,384]{1,0:T(8,128)(2,1)} %get-tuple-element.63.keys, bf16[640,384]{1,0:T(8,128)(2,1)} %get-tuple-element.64.values), custom_call_target="tpu_custom_call" | custom-call | flops 1677721600 | bytes 2457600 | tf_op jit(solution)/shard_map/suffix/pallas_call | solution.py:376
  279.9 0.8 copy-done.7
  280.7 36.1 %prefix.2 = (bf16[640,512]{1,0:T(8,128)(2,1)}, bf16[640,512]{1,0:T(8,128)(2,1)}) custom-call(s32[8]{0:T(128)} %reshape_squeeze.6.starts, s32[8]{0:T(128)} %reshape_squeeze.7.lengths, bf16[640,384]{1,0:T(8,128)(2,1)} %get-tuple-element.60.refs_0_.queries, bf16[640,384]{1,0:T(8,128)(2,1)} %copy-done.7, bf16[2,2048,768]{2,1,0:T(8,128)(2,1)} %refs_2_.3, ...), custom_call_target="tpu_custom_call" | custom-call | flops 5368709120 | bytes 12582912 | tf_op jit(solution)/shard_map/prefix/pallas_call | solution.py:309
  316.8 7.6 %suffix.3 = (f32[640,384]{1,0:T(8,128)}, f32[640,128]{1,0:T(8,128)}) custom-call(s32[640,1]{1,0:T(8,128)} %reduce_sum.116.row_start, bf16[640,384]{1,0:T(8,128)(2,1)} %get-tuple-element.69.refs_0_.queries, bf16[640,384]{1,0:T(8,128)(2,1)} %get-tuple-element.72.keys, bf16[640,384]{1,0:T(8,128)(2,1)} %get-tuple-element.73.values), custom_call_target="tpu_custom_call" | custom-call | flops 1677721600 | bytes 2457600 | tf_op jit(solution)/shard_map/suffix/pallas_call | solution.py:376
  324.4 0.8 copy-done.6
  325.2 24.1 %prefix.3 = (bf16[640,512]{1,0:T(8,128)(2,1)}, bf16[640,512]{1,0:T(8,128)(2,1)}) custom-call(s32[8]{0:T(128)} %reshape_squeeze.6.starts, s32[8]{0:T(128)} %reshape_squeeze.7.lengths, bf16[640,384]{1,0:T(8,128)(2,1)} %get-tuple-element.69.refs_0_.queries, bf16[640,384]{1,0:T(8,128)(2,1)} %copy-done.6, bf16[2,2048,768]{2,1,0:T(8,128)(2,1)} %refs_2_.3, ...), custom_call_target="tpu_custom_call" | custom-call | flops 5368709120 | bytes 12582912 | tf_op jit(solution)/shard_map/prefix/pallas_call | solution.py:309
  349.3 0.8 copy-done.5
  350.2 3.6 merge.2
  354.3 4.1 maximum_select_fusion
  358.5 37.2 %pad_maximum_fusion = bf16[1536,3072]{1,0:T(8,128)(2,1)} fusion(bf16[768,3072]{1,0:T(8,128)(2,1)S(1)} %maximum_select_fusion, bf16[768,768]{1,0:T(8,128)(2,1)S(1)} %get-tuple-element.119, bf16[768,768]{1,0:T(8,128)(2,1)S(1)} %copy-done.2, bf16[768,768]{1,0:T(8,128)(2,1)S(1)} %get-tuple-element.114, bf16[768,768]{1,0:T(8,128)(2,1)S(1)} %get-tuple-element.113), kind=kLoop, calls=%fused_computation | loop fusion | flops 47185920 | bytes 18874368 | tf_op jit(solution)/shard_map/concatenate | solution.py:544
  395.7 0.8 copy-done.4
  396.5 3.6 merge.3
  400.1 1.5 collective-permute-start.16
  401.6 12.1 %collective-permute-done.16 = bf16[640,384]{1,0:T(8,128)(2,1)S(1)} collective-permute-done((bf16[640,384]{1,0:T(8,128)(2,1)}, bf16[640,384]{1,0:T(8,128)(2,1)S(1)}, u32[]{:S(2)}, u32[]{:S(2)}) %collective-permute-start.16) | collective-permute-done | bytes 491552 | tf_op jit(solution)/shard_map/ppermute | solution.py:466
  413.7 9.2 %fusion.3 = f32[640,3072]{1,0:T(8,128)S(1)} fusion(bf16[1536,3072]{1,0:T(8,128)(2,1)} %pad_maximum_fusion, bf16[640,384]{1,0:T(8,128)(2,1)S(1)} %collective-permute-done.16, bf16[640,384]{1,0:T(8,128)(2,1)} %collective-permute-done.15, bf16[640,384]{1,0:T(8,128)(2,1)} %merge.3, bf16[640,384]{1,0:T(8,128)(2,1)} %merge.2), kind=kOutput, calls=%fused_computation.9 | convolution fusion | flops 6047662080 | bytes 19267584 | tf_op jit(solution)/shard_map/dot_general | solution.py:564
  422.9 3.1 copy-done
  426.2 1.5 collective-permute-start.17
  427.7 1.5 collective-permute-start.18
  429.3 1.3 collective-permute-start.23
  431.2 10.9 %collective-permute-done.17 = bf16[320,768]{1,0:T(8,128)(2,1)S(1)} collective-permute-done((bf16[320,768]{1,0:T(8,128)(2,1)S(1)}, bf16[320,768]{1,0:T(8,128)(2,1)S(1)}, u32[]{:S(2)}, u32[]{:S(2)}) %collective-permute-start.17) | collective-permute-done | bytes 491552 | tf_op jit(solution)/shard_map/ppermute | solution.py:589
  442.2 2.6 add_convert_fusion.6
  444.8 4.5 collective-permute-start.19
  449.3 1.3 collective-permute-start.20
  450.6 2.1 collective-permute-done.23
  452.7 10.2 %collective-permute-done.19 = bf16[320,768]{1,0:T(8,128)(2,1)S(1)} collective-permute-done((bf16[320,768]{1,0:T(8,128)(2,1)}, bf16[320,768]{1,0:T(8,128)(2,1)S(1)}, u32[]{:S(2)}, u32[]{:S(2)}) %collective-permute-start.19) | collective-permute-done | bytes 491552 | tf_op jit(solution)/shard_map/ppermute | solution.py:589
  463.5 2.7 add_convert_fusion.4
  466.2 4.0 collective-permute-start.25
  470.2 1.3 collective-permute-start.26
  471.5 4.6 collective-permute-start.21
  476.0 1.9 collective-permute-start.22
  478.0 4.4 collective-permute-done.25
  482.4 3.9 collective-permute-done.26
  486.2 1.8 add_convert_fusion
  488.0 1.9 collective-permute-start.27
  489.9 4.7 collective-permute-start.28
  494.8 2.1 collective-permute-done.22
  496.9 4.8 collective-permute-done.27
  501.7 4.1 collective-permute-done.28
  505.8 2.4 fusion.12
  508.2 1.0 pad_maximum_fusion.1
  (90 shorter events, 12.9 us)
Async XLA Ops:
  6.5 162.8 %all-gather.2.cloned.1.call-start = ((), (), s32[]{:S(2)}) async-start(), calls=%async_computation | async-start | bytes 8847360 | tf_op jit(solution)/shard_map/all_gather | solution.py:470
  7.3 7.0 %copy-start.1 = (bf16[1536,2304]{1,0:T(8,128)(2,1)S(1)}, bf16[1536,2304]{1,0:T(8,128)(2,1)}, u32[]{:S(2)}) copy-start(bf16[1536,2304]{1,0:T(8,128)(2,1)} %param.15) | copy-start | bytes 21233668
  8.1 4.8 collective-permute-start
  12.9 81.3 %copy-start.13 = (s32[1,8]{1,0:T(1,128)S(1)}, s32[1,8]{1,0:T(1,128)}, u32[]{:S(2)}) copy-start(s32[1,8]{1,0:T(1,128)} %param.22) | copy-start | bytes 100
  12.9 81.4 %copy-start.9 = (s32[1,8]{1,0:T(1,128)S(1)}, s32[1,8]{1,0:T(1,128)}, u32[]{:S(2)}) copy-start(s32[1,8]{1,0:T(1,128)} %param.21) | copy-start | bytes 100
  13.0 81.7 %copy-start.10 = (s32[2,8]{1,0:T(2,128)}, s32[2,8]{1,0:T(2,128)S(1)}, u32[]{:S(2)}) copy-start(s32[2,8]{1,0:T(2,128)S(1)} %collective-permute-done) | copy-start | bytes 196
  13.0 78.3 %collective-permute-start.2 = (bf16[1536,1152]{1,0:T(8,128)(2,1)}, bf16[1536,1152]{1,0:T(8,128)(2,1)}, u32[]{:S(2)}, u32[]{:S(2)}) collective-permute-start(bf16[1536,1152]{1,0:T(8,128)(2,1)} %slice.39.refs_0_), channel_id=1, source_target_pairs={{0,16},{8,24},{16,0},{24,8},{1,17},{9,25},{17,1},{25,9},{2,18},{10... | collective-permute-start | bytes 10616840 | tf_op jit(solution)/shard_map/ppermute | solution.py:459
  14.2 88.5 %collective-permute-start.1 = (bf16[1536,1152]{1,0:T(8,128)(2,1)}, bf16[1536,1152]{1,0:T(8,128)(2,1)}, u32[]{:S(2)}, u32[]{:S(2)}) collective-permute-start(bf16[1536,1152]{1,0:T(8,128)(2,1)} %slice.39.refs_0_), channel_id=1, source_target_pairs={{0,8},{8,0},{16,24},{24,16},{1,9},{9,1},{17,25},{25,17},{2,10},{10... | collective-permute-start | bytes 10616840 | tf_op jit(solution)/shard_map/ppermute | solution.py:456
  91.2 77.3 %collective-permute-start.9 = (bf16[1536,1152]{1,0:T(8,128)(2,1)}, bf16[1536,1152]{1,0:T(8,128)(2,1)}, u32[]{:S(2)}, u32[]{:S(2)}) collective-permute-start(bf16[1536,1152]{1,0:T(8,128)(2,1)} %slice.47.refs_0_), channel_id=1, source_target_pairs={{0,16},{8,24},{16,0},{24,8},{1,17},{9,25},{17,1},{25,9},{2,18},{10... | collective-permute-start | bytes 10616840 | tf_op jit(solution)/shard_map/ppermute | solution.py:459
  92.5 76.8 %collective-permute-start.3 = (bf16[1536,1152]{1,0:T(8,128)(2,1)}, bf16[1536,1152]{1,0:T(8,128)(2,1)}, u32[]{:S(2)}, u32[]{:S(2)}) collective-permute-start(bf16[1536,1152]{1,0:T(8,128)(2,1)} %collective-permute-done.2.refs_2_), channel_id=1, source_target_pairs={{0,8},{8,0},{16,24},{24,16},{1,9},{9,1},{17,25},{25,17},{2,10},{10... | collective-permute-start | bytes 10616840 | tf_op jit(solution)/shard_map/ppermute | solution.py:456
  92.5 187.3 %collective-permute-start.5 = (bf16[2,2048,768]{2,1,0:T(8,128)(2,1)}, bf16[2,2048,768]{2,1,0:T(8,128)(2,1)}, u32[]{:S(2)}, u32[]{:S(2)}) collective-permute-start(bf16[2,2048,768]{2,1,0:T(8,128)(2,1)} %refs_2_.3), channel_id=1, source_target_pairs={{0,8},{8,0},{16,24},{24,16},{1,9},{9,1},{17,25},{25,17},{2,10},{10... | collective-permute-start | bytes 18874376 | tf_op jit(solution)/shard_map/ppermute | solution.py:456
  93.0 186.8 %collective-permute-start.6 = (bf16[2,2048,768]{2,1,0:T(8,128)(2,1)}, bf16[2,2048,768]{2,1,0:T(8,128)(2,1)}, u32[]{:S(2)}, u32[]{:S(2)}) collective-permute-start(bf16[2,2048,768]{2,1,0:T(8,128)(2,1)} %refs_4_.3), channel_id=1, source_target_pairs={{0,8},{8,0},{16,24},{24,16},{1,9},{9,1},{17,25},{25,17},{2,10},{10... | collective-permute-start | bytes 18874376 | tf_op jit(solution)/shard_map/ppermute | solution.py:456
  100.1 69.8 %copy-start.11 = (f32[96]{0:T(128)S(1)}, f32[96]{0:T(128)}, u32[]{:S(2)}) copy-start(f32[96]{0:T(128)} %pad.20.clone) | copy-start | bytes 1156
  100.1 69.8 %copy-start.12 = (f32[96]{0:T(128)S(1)}, f32[96]{0:T(128)}, u32[]{:S(2)}) copy-start(f32[96]{0:T(128)} %pad.23.clone) | copy-start | bytes 1156
  102.8 143.9 %collective-permute-start.8 = (bf16[1536,1152]{1,0:T(8,128)(2,1)}, bf16[1536,1152]{1,0:T(8,128)(2,1)}, u32[]{:S(2)}, u32[]{:S(2)}) collective-permute-start(bf16[1536,1152]{1,0:T(8,128)(2,1)} %slice.47.refs_0_), channel_id=1, source_target_pairs={{0,8},{8,0},{16,24},{24,16},{1,9},{9,1},{17,25},{25,17},{2,10},{10... | collective-permute-start | bytes 10616840 | tf_op jit(solution)/shard_map/ppermute | solution.py:456
  168.5 79.7 %collective-permute-start.10 = (bf16[1536,1152]{1,0:T(8,128)(2,1)}, bf16[1536,1152]{1,0:T(8,128)(2,1)}, u32[]{:S(2)}, u32[]{:S(2)}) collective-permute-start(bf16[1536,1152]{1,0:T(8,128)(2,1)} %collective-permute-done.9.refs_2_), channel_id=1, source_target_pairs={{0,8},{8,0},{16,24},{24,16},{1,9},{9,1},{17,25},{25,17},{2,10},{10... | collective-permute-start | bytes 10616840 | tf_op jit(solution)/shard_map/ppermute | solution.py:456
  169.4 54.0 %collective-permute-start.13 = (bf16[768,1536]{1,0:T(8,128)(2,1)}, bf16[768,1536]{1,0:T(8,128)(2,1)}, u32[]{:S(2)}, u32[]{:S(2)}) collective-permute-start(bf16[768,1536]{1,0:T(8,128)(2,1)} %fusion.2), channel_id=1, source_target_pairs={{0,1},{1,0},{2,3},{3,2},{4,5},{5,4},{6,7},{7,6},{8,9},{9,8},{10,11... | collective-permute-start | bytes 7077896 | tf_op jit(solution)/shard_map/ppermute | solution.py:466
  223.3 131.0 %collective-permute-start.14 = (bf16[768,1536]{1,0:T(8,128)(2,1)}, bf16[768,1536]{1,0:T(8,128)(2,1)S(1)}, u32[]{:S(2)}, u32[]{:S(2)}) collective-permute-start(bf16[768,1536]{1,0:T(8,128)(2,1)} %collective-permute-done.13), channel_id=1, source_target_pairs={{0,8},{8,0},{16,24},{24,16},{1,9},{9,1},{17,25},{25,17},{2,10},{10... | collective-permute-start | bytes 7077896 | tf_op jit(solution)/shard_map/ppermute | solution.py:456
  246.7 33.2 %collective-permute-start.4 = (bf16[640,384]{1,0:T(8,128)(2,1)}, bf16[640,384]{1,0:T(8,128)(2,1)S(1)}, u32[]{:S(2)}, u32[]{:S(2)}) collective-permute-start(bf16[640,384]{1,0:T(8,128)(2,1)} %get-tuple-element.60.refs_0_.queries), channel_id=1, source_target_pairs={{0,16},{8,24},{16,0},{24,8},{1,17},{9,25},{17,1},{25,9},{2,18},{10... | collective-permute-start | bytes 1474568 | tf_op jit(solution)/shard_map/ppermute | solution.py:459
  271.5 52.9 %collective-permute-start.11 = (bf16[640,384]{1,0:T(8,128)(2,1)}, bf16[640,384]{1,0:T(8,128)(2,1)S(1)}, u32[]{:S(2)}, u32[]{:S(2)}) collective-permute-start(bf16[640,384]{1,0:T(8,128)(2,1)} %get-tuple-element.69.refs_0_.queries), channel_id=1, source_target_pairs={{0,16},{8,24},{16,0},{24,8},{1,17},{9,25},{17,1},{25,9},{2,18},{10... | collective-permute-start | bytes 1474568 | tf_op jit(solution)/shard_map/ppermute | solution.py:459
  279.9 0.8 copy-start.7
  316.8 32.6 %collective-permute-start.7 = (bf16[640,512]{1,0:T(8,128)(2,1)}, bf16[640,512]{1,0:T(8,128)(2,1)S(1)}, u32[]{:S(2)}, u32[]{:S(2)}) collective-permute-start(bf16[640,512]{1,0:T(8,128)(2,1)} %get-tuple-element.62), channel_id=1, source_target_pairs={{0,16},{8,24},{16,0},{24,8},{1,17},{9,25},{17,1},{25,9},{2,18},{10... | collective-permute-start | bytes 1966088 | tf_op jit(solution)/shard_map/ppermute | solution.py:459
  324.4 0.8 copy-start.6
  349.2 46.4 %collective-permute-start.12 = (bf16[640,512]{1,0:T(8,128)(2,1)}, bf16[640,512]{1,0:T(8,128)(2,1)S(1)}, u32[]{:S(2)}, u32[]{:S(2)}) collective-permute-start(bf16[640,512]{1,0:T(8,128)(2,1)} %get-tuple-element.71), channel_id=1, source_target_pairs={{0,16},{8,24},{16,0},{24,8},{1,17},{9,25},{17,1},{25,9},{2,18},{10... | collective-permute-start | bytes 1966088 | tf_op jit(solution)/shard_map/ppermute | solution.py:459
  349.3 0.8 copy-start.5
  353.8 4.7 copy-start.2
  353.8 47.8 %collective-permute-start.15 = (bf16[640,384]{1,0:T(8,128)(2,1)}, bf16[640,384]{1,0:T(8,128)(2,1)}, u32[]{:S(2)}, u32[]{:S(2)}) collective-permute-start(bf16[640,384]{1,0:T(8,128)(2,1)} %merge.2), channel_id=1, source_target_pairs={{0,1},{1,0},{2,3},{3,2},{4,5},{5,4},{6,7},{7,6},{8,9},{9,8},{10,11... | collective-permute-start | bytes 1474568 | tf_op jit(solution)/shard_map/ppermute | solution.py:466
  395.7 0.8 copy-start.4
  400.1 13.6 %collective-permute-start.16 = (bf16[640,384]{1,0:T(8,128)(2,1)}, bf16[640,384]{1,0:T(8,128)(2,1)S(1)}, u32[]{:S(2)}, u32[]{:S(2)}) collective-permute-start(bf16[640,384]{1,0:T(8,128)(2,1)} %merge.3), channel_id=1, source_target_pairs={{0,1},{1,0},{2,3},{3,2},{4,5},{5,4},{6,7},{7,6},{8,9},{9,8},{10,11... | collective-permute-start | bytes 1474568 | tf_op jit(solution)/shard_map/ppermute | solution.py:466
  422.9 3.1 copy-start
  426.2 15.9 %collective-permute-start.17 = (bf16[320,768]{1,0:T(8,128)(2,1)S(1)}, bf16[320,768]{1,0:T(8,128)(2,1)S(1)}, u32[]{:S(2)}, u32[]{:S(2)}) collective-permute-start(bf16[320,768]{1,0:T(8,128)(2,1)S(1)} %get-tuple-element.79), channel_id=1, source_target_pairs={{0,2},{1,3},{8,10},{9,11},{16,18},{17,19},{24,26},{25,27}} | collective-permute-start | bytes 1474568 | tf_op jit(solution)/shard_map/ppermute | solution.py:589
  427.7 14.4 %collective-permute-start.18 = (bf16[320,768]{1,0:T(8,128)(2,1)S(1)}, bf16[320,768]{1,0:T(8,128)(2,1)}, u32[]{:S(2)}, u32[]{:S(2)}) collective-permute-start(bf16[320,768]{1,0:T(8,128)(2,1)S(1)} %get-tuple-element.80), channel_id=1, source_target_pairs={{6,4},{7,5},{14,12},{15,13},{22,20},{23,21},{30,28},{31,29}} | collective-permute-start | bytes 1474568 | tf_op jit(solution)/shard_map/ppermute | solution.py:589
  429.3 23.4 %collective-permute-start.23 = (bf16[320,768]{1,0:T(8,128)(2,1)S(1)}, bf16[320,768]{1,0:T(8,128)(2,1)S(1)}, u32[]{:S(2)}, u32[]{:S(2)}) collective-permute-start(bf16[320,768]{1,0:T(8,128)(2,1)S(1)} %get-tuple-element.91), channel_id=1, source_target_pairs={{0,2},{1,3},{8,10},{9,11},{16,18},{17,19},{24,26},{25,27}} | collective-permute-start | bytes 1474568 | tf_op jit(solution)/shard_map/ppermute | solution.py:589
  430.5 22.1 %collective-permute-start.24 = (bf16[320,768]{1,0:T(8,128)(2,1)S(1)}, bf16[320,768]{1,0:T(8,128)(2,1)S(1)}, u32[]{:S(2)}, u32[]{:S(2)}) collective-permute-start(bf16[320,768]{1,0:T(8,128)(2,1)S(1)} %get-tuple-element.92), channel_id=1, source_target_pairs={{6,4},{7,5},{14,12},{15,13},{22,20},{23,21},{30,28},{31,29}} | collective-permute-start | bytes 1474568 | tf_op jit(solution)/shard_map/ppermute | solution.py:589
  444.8 18.1 %collective-permute-start.19 = (bf16[320,768]{1,0:T(8,128)(2,1)}, bf16[320,768]{1,0:T(8,128)(2,1)S(1)}, u32[]{:S(2)}, u32[]{:S(2)}) collective-permute-start(bf16[320,768]{1,0:T(8,128)(2,1)} %get-tuple-element.83), channel_id=1, source_target_pairs={{0,2},{1,3},{2,4},{3,5},{8,10},{9,11},{10,12},{11,13},{16,18},{17,... | collective-permute-start | bytes 1474568 | tf_op jit(solution)/shard_map/ppermute | solution.py:589
  449.3 14.2 %collective-permute-start.20 = (bf16[320,768]{1,0:T(8,128)(2,1)S(1)}, bf16[320,768]{1,0:T(8,128)(2,1)}, u32[]{:S(2)}, u32[]{:S(2)}) collective-permute-start(bf16[320,768]{1,0:T(8,128)(2,1)S(1)} %get-tuple-element.84), channel_id=1, source_target_pairs={{4,2},{5,3},{6,4},{7,5},{12,10},{13,11},{14,12},{15,13},{20,18},{2... | collective-permute-start | bytes 1474568 | tf_op jit(solution)/shard_map/ppermute | solution.py:589
  466.2 28.5 %copy-start.8 = (bf16[768]{0:T(1024)(128)(2,1)S(1)}, bf16[768]{0:T(1024)(128)(2,1)}, u32[]{:S(2)}) copy-start(bf16[768]{0:T(1024)(128)(2,1)} %param.18) | copy-start | bytes 4612
  466.2 28.5 %copy-start.3 = (bf16[640,768]{1,0:T(8,128)(2,1)S(1)}, bf16[640,768]{1,0:T(8,128)(2,1)}, u32[]{:S(2)}) copy-start(bf16[640,768]{1,0:T(8,128)(2,1)} %param.12) | copy-start | bytes 2949124
  466.2 16.2 %collective-permute-start.25 = (bf16[320,768]{1,0:T(8,128)(2,1)S(1)}, bf16[320,768]{1,0:T(8,128)(2,1)S(1)}, u32[]{:S(2)}, u32[]{:S(2)}) collective-permute-start(bf16[320,768]{1,0:T(8,128)(2,1)S(1)} %get-tuple-element.97), channel_id=1, source_target_pairs={{0,2},{1,3},{2,4},{3,5},{8,10},{9,11},{10,12},{11,13},{16,18},{17,... | collective-permute-start | bytes 1474568 | tf_op jit(solution)/shard_map/ppermute | solution.py:589
  470.2 16.1 %collective-permute-start.26 = (bf16[320,768]{1,0:T(8,128)(2,1)S(1)}, bf16[320,768]{1,0:T(8,128)(2,1)S(1)}, u32[]{:S(2)}, u32[]{:S(2)}) collective-permute-start(bf16[320,768]{1,0:T(8,128)(2,1)S(1)} %get-tuple-element.98), channel_id=1, source_target_pairs={{4,2},{5,3},{6,4},{7,5},{12,10},{13,11},{14,12},{15,13},{20,18},{2... | collective-permute-start | bytes 1474568 | tf_op jit(solution)/shard_map/ppermute | solution.py:589
  471.5 23.3 %collective-permute-start.21 = (bf16[320,768]{1,0:T(8,128)(2,1)S(1)}, bf16[320,768]{1,0:T(8,128)(2,1)S(1)}, u32[]{:S(2)}, u32[]{:S(2)}) collective-permute-start(bf16[320,768]{1,0:T(8,128)(2,1)S(1)} %get-tuple-element.87), channel_id=1, source_target_pairs={{0,2},{1,3},{2,4},{3,5},{4,6},{5,7},{8,10},{9,11},{10,12},{11,13},... | collective-permute-start | bytes 1474568 | tf_op jit(solution)/shard_map/ppermute | solution.py:589
  476.0 20.8 %collective-permute-start.22 = (bf16[320,768]{1,0:T(8,128)(2,1)S(1)}, bf16[320,768]{1,0:T(8,128)(2,1)}, u32[]{:S(2)}, u32[]{:S(2)}) collective-permute-start(bf16[320,768]{1,0:T(8,128)(2,1)S(1)} %get-tuple-element.88), channel_id=1, source_target_pairs={{2,0},{3,1},{4,2},{5,3},{6,4},{7,5},{10,8},{11,9},{12,10},{13,11},... | collective-permute-start | bytes 1474568 | tf_op jit(solution)/shard_map/ppermute | solution.py:589
  488.0 13.7 %collective-permute-start.27 = (bf16[320,768]{1,0:T(8,128)(2,1)S(1)}, bf16[320,768]{1,0:T(8,128)(2,1)}, u32[]{:S(2)}, u32[]{:S(2)}) collective-permute-start(bf16[320,768]{1,0:T(8,128)(2,1)S(1)} %get-tuple-element.103), channel_id=1, source_target_pairs={{0,2},{1,3},{2,4},{3,5},{4,6},{5,7},{8,10},{9,11},{10,12},{11,13},... | collective-permute-start | bytes 1474568 | tf_op jit(solution)/shard_map/ppermute | solution.py:589
  489.9 15.9 %collective-permute-start.28 = (bf16[320,768]{1,0:T(8,128)(2,1)S(1)}, bf16[320,768]{1,0:T(8,128)(2,1)}, u32[]{:S(2)}, u32[]{:S(2)}) collective-permute-start(bf16[320,768]{1,0:T(8,128)(2,1)S(1)} %get-tuple-element.104), channel_id=1, source_target_pairs={{2,0},{3,1},{4,2},{5,3},{6,4},{7,5},{10,8},{11,9},{12,10},{13,11},... | collective-permute-start | bytes 1474568 | tf_op jit(solution)/shard_map/ppermute | solution.py:589
Sparse Core Ops, SparseCore 0:
  9.5 117.5 all-gather.1
